TPU v7x, 32 devices: a whole 2x2x4 slice. The times are simulated.
32 devices in a mesh: wide: 8 (over z, core), narrow: 4 (over y, x).
Axes of the slice: x: 2, y: 2, z: 4, core: 2. Of those that a mesh axis runs over, the one named last changes fastest.
Arguments:
- obs: bfloat16 [1536, 128], P(('wide', 'narrow')), may hold values from -6 to 6
- actions: float32 [1536, 5, 8], P(('wide', 'narrow')), may hold values from -1 to 1
- target_latents: float32 [1536, 5, 768], P(('wide', 'narrow')), may hold values from 0 to 0.25
- noise: float32 [1536, 5, 8], P(('wide', 'narrow')), may hold values from -3 to 3
- horizon: int32 [1536], P(('wide', 'narrow')), may hold values from 3 to 5, as said below
- step_mask: int32 [1536, 5], P(('wide', 'narrow')), may hold values 0 or 1
- task_ids: int32 [1536], P(('wide', 'narrow')), may hold values from 0 to 79
- reward_bins: int32 [1536, 5], P(('wide', 'narrow')), may hold values from 0 to 100
- value_bins: int32 [1536, 5], P(('wide', 'narrow')), may hold values from 0 to 100
- task_table: float32 [80, 96], replicated, may hold values from -4 to 4
- encoder_first: bfloat16 [128, 1024], P('narrow'), may hold values from -0.5 to 0.5
- encoder_second: bfloat16 [1024, 768], P('narrow'), may hold values from -0.1875 to 0.1875
- dynamics_first: bfloat16 [872, 1024], P('narrow'), may hold values from -0.21875 to 0.21875
- dynamics_second: bfloat16 [1024, 1024], P('narrow'), may hold values from -0.1875 to 0.1875
- dynamics_third: bfloat16 [1024, 768], P('narrow'), may hold values from -0.1875 to 0.1875
- reward_first: bfloat16 [872, 1024], P('narrow'), may hold values from -0.21875 to 0.21875
- reward_second: bfloat16 [1024, 1024], P('narrow'), may hold values from -0.1875 to 0.1875
- reward_third: bfloat16 [1024, 101], P('narrow'), may hold values from -0.1875 to 0.1875
- critic_first: bfloat16 [5, 872, 1024], P(None, 'narrow'), may hold values from -0.21875 to 0.21875
- critic_second: bfloat16 [5, 1024, 1024], P(None, 'narrow'), may hold values from -0.1875 to 0.1875
- critic_third: bfloat16 [5, 1024, 101], P(None, 'narrow'), may hold values from -0.1875 to 0.1875
- policy_first: bfloat16 [864, 1024], P('narrow'), may hold values from -0.21875 to 0.21875
- policy_second: bfloat16 [1024, 1024], P('narrow'), may hold values from -0.1875 to 0.1875
- policy_third: bfloat16 [1024, 16], P('narrow'), may hold values from -0.1875 to 0.1875
- encoder_bias: float32 [1792], replicated, may hold values from -1.5 to 1.5
- encoder_gain: float32 [1024], replicated, may hold values from 0.25 to 1.75
- dynamics_bias: float32 [2816], replicated, may hold values from -1.5 to 1.5
- dynamics_gain: float32 [2048], replicated, may hold values from 0.25 to 1.75
- reward_bias: float32 [2149], replicated, may hold values from -1.5 to 1.5
- reward_gain: float32 [2048], replicated, may hold values from 0.25 to 1.75
- critic_bias: float32 [5, 2149], replicated, may hold values from -1.5 to 1.5
- critic_gain: float32 [5, 2048], replicated, may hold values from 0.25 to 1.75
- policy_bias: float32 [2064], replicated, may hold values from -1.5 to 1.5
- policy_gain: float32 [2048], replicated, may hold values from 0.25 to 1.75
Outputs:
- row_loss: float32 [1536], P(('wide', 'narrow'))
- latents: float32 [1536, 5, 768], P(('wide', 'narrow'))
- obs_grad: float32 [1536, 128], P(('wide', 'narrow'))
- grad_task_table: float32 [80, 96], replicated
- grad_encoder_first: float32 [128, 1024], P('narrow')
- grad_encoder_second: float32 [1024, 768], P('narrow')
- grad_dynamics_first: float32 [872, 1024], P('narrow')
- grad_dynamics_second: float32 [1024, 1024], P('narrow')
- grad_dynamics_third: float32 [1024, 768], P('narrow')
- grad_reward_first: float32 [872, 1024], P('narrow')
- grad_reward_second: float32 [1024, 1024], P('narrow')
- grad_reward_third: float32 [1024, 101], P('narrow')
- grad_critic_first: float32 [5, 872, 1024], P(None, 'narrow')
- grad_critic_second: float32 [5, 1024, 1024], P(None, 'narrow')
- grad_critic_third: float32 [5, 1024, 101], P(None, 'narrow')
- grad_policy_first: float32 [864, 1024], P('narrow')
- grad_policy_second: float32 [1024, 1024], P('narrow')
- grad_policy_third: float32 [1024, 16], P('narrow')
- grad_encoder_bias: float32 [1792], replicated
- grad_encoder_gain: float32 [1024], replicated
- grad_dynamics_bias: float32 [2816], replicated
- grad_dynamics_gain: float32 [2048], replicated
- grad_reward_bias: float32 [2149], replicated
- grad_reward_gain: float32 [2048], replicated
- grad_critic_bias: float32 [5, 2149], replicated
- grad_critic_gain: float32 [5, 2048], replicated
- grad_policy_bias: float32 [2064], replicated
- grad_policy_gain: float32 [2048], replicated
Inputs may be any that keep to these rules, and one draw needn't show every extreme that they name: Each transition's horizon is 3 or 5.
All inputs are finite; a program needn't handle non-finite values. No bound on the sum of `step_mask` on one device may be relied on, other than what follows from the above.
Results may differ from a plain program's by a relative error of at most 0.018.
Values may be sent and summed in bfloat16 or wider, within the bound.
No kernel may reach another device: no remote copies, remote signals or barrier semaphores. Data moves between devices by JAX's collectives and lax.ppermute only.
A program may use at most 448 MiB of HBM per device.

v0:
```python
import functools
import math

import jax
import jax.numpy as jnp
from jax import lax
from jax.experimental import pallas as pl
from jax.experimental.pallas import tpu as pltpu
from jax.sharding import PartitionSpec as P

F32 = jnp.float32
BF16 = jnp.bfloat16
SLOTS = 8
SLOT_HEAD = (0, 1, 0, 1, 2, 3, 4, 0)
SLOT_PROBE = (0, 0, 1, 1, 0, 0, 0, 0)
SLOT_REWARD = (0, 0, 0, 0, 0, 0, 0, 1)
HEAD_SLOT = (0, 1, 4, 5, 6)
REWARD_SLOT = 7
CHOSEN, RBIN, VBIN, WEIGHT = 104, 112, 113, 114
WIDTH = 896
VMEM = pltpu.MemorySpace.VMEM


def dot(a, b):
    return jnp.dot(a, b, preferred_element_type=F32)


def dot_nt(a, b):
    return lax.dot_general(a, b, (((1,), (1,)), ((), ())), preferred_element_type=F32)


def dot_tn(a, b):
    return lax.dot_general(a, b, (((0,), (0,)), ((), ())), preferred_element_type=F32)


def norm_mish(pre, gain):
    center = pre - jnp.mean(pre, axis=-1, keepdims=True)
    scale = lax.rsqrt(jnp.mean(center * center, axis=-1, keepdims=True) + 1e-05)
    normed = center * scale
    v = normed * gain
    e = jnp.exp(jnp.minimum(v, 20.0))
    n = e * (e + 2.0)
    r = 1.0 / (n + 2.0)
    t = n * r
    return v * t, normed, t + v * (4.0 * e * (1.0 + e)) * (r * r), scale


def norm_mish_back(upstream, normed, slope, scale, gain):
    dv = upstream * slope
    gain_grad = jnp.sum(dv * normed, axis=0, keepdims=True)
    a = dv * gain
    dpre = scale * (
        a
        - jnp.mean(a, axis=-1, keepdims=True)
        - normed * jnp.mean(a * normed, axis=-1, keepdims=True)
    )
    return dpre, gain_grad, jnp.sum(dpre, axis=0, keepdims=True)


def lanes(shape):
    return lax.broadcasted_iota(jnp.int32, shape, len(shape) - 1)


def column(block, at):
    return jnp.sum(jnp.where(lanes(block.shape) == at, block, 0.0), axis=-1, keepdims=True)


def eights(block, join):
    lane = lanes(block.shape)
    for step in (1, 2, 4):
        partner = jnp.where(
            (lane & step) == 0, pltpu.roll(block, 128 - step, 1), pltpu.roll(block, step, 1)
        )
        block = join(block, partner)
    return block


def by_block(fn, *arrays):
    pieces = []
    for start in range(0, arrays[0].shape[1], 128):
        pieces.append(fn(*(a[:, start : start + 128] for a in arrays)))
    return jnp.concatenate(pieces, axis=1)


def simnorm_block(pre):
    e = jnp.exp(pre - eights(pre, jnp.maximum))
    return e / eights(e, jnp.add)


def simnorm_back_block(latent, upstream):
    return latent * (upstream - eights(latent * upstream, jnp.add))


VEC = {
    name: at
    for at, name in enumerate(
        ("eb1", "eg1", "eb2", "db1", "dg1", "db2", "dg2", "db3", "pb1", "pg1", "pb2", "pg2", "pb3")
    )
}


def forward_kernel(
    steps, obs, side, noise, target, vec, e1, e2, d1, d2, d3, p1, p2, p3,
    xg, z0, z, rowloss, e_h, e_n, e_s, e_r, d_h1, d_n1, d_s1, d_r1, d_h2, d_n2, d_s2, d_r2,
    p_h1, p_n1, p_s1, p_r1, p_h2, p_n2, p_s2, p_r2, pout,
):
    rows = obs.shape[0]
    lat = z0.shape[1]

    def v(name, width=1024):
        return vec[VEC[name] : VEC[name] + 1, :width]

    def layer(x, w, bias, gain, h, n, s, r, at):
        out, normed, slope, scale = norm_mish(dot(x, w) + v(bias), v(gain))
        low = out.astype(BF16)
        h[at, :] = low
        n[at, :] = normed
        s[at, :] = slope
        r[at, :] = scale
        return low

    everything = slice(0, rows)
    x1 = layer(obs[...], e1[...], "eb1", "eg1", e_h, e_n, e_s, e_r, everything)
    latent = by_block(simnorm_block, dot(x1, e2[...]) + v("eb2", lat))
    z0[...] = latent
    xg[:, lat:] = side[...]
    for t in range(steps):
        at = slice(t * rows, (t + 1) * rows)
        xg[at, :lat] = latent.astype(BF16)
        h1 = layer(xg[at, :], d1[...], "db1", "dg1", d_h1, d_n1, d_s1, d_r1, at)
        h2 = layer(h1, d2[...], "db2", "dg2", d_h2, d_n2, d_s2, d_r2, at)
        latent = by_block(simnorm_block, dot(h2, d3[...]) + v("db3", lat))
        z[at, :] = latent
    whole = slice(0, steps * rows)
    h1 = layer(xg[...], p1[...], "pb1", "pg1", p_h1, p_n1, p_s1, p_r1, whole)
    h2 = layer(h1, p2[...], "pb2", "pg2", p_h2, p_n2, p_s2, p_r2, whole)
    out = dot(h2, p3[...]) + v("pb3", 256)
    pout[...] = out
    mu, raw = out[:, :128], out[:, 128:]
    eps = noise[...]
    log_std = -10.0 + 6.0 * (jnp.tanh(raw) + 1.0)
    moved = mu + jnp.exp(log_std) * eps
    chosen = jnp.tanh(moved)
    bent = -2.0 * moved
    soft = jnp.maximum(bent, 0.0) + jnp.log1p(jnp.exp(-jnp.abs(bent)))
    density = -0.5 * eps * eps - log_std - 0.5 * math.log(2.0 * math.pi)
    terms = density - 2.0 * (math.log(2.0) - moved - soft)
    valid = lanes(terms.shape) < 8
    log_prob = jnp.sum(jnp.where(valid, terms, 0.0), axis=-1, keepdims=True)
    low = pltpu.roll(jnp.where(valid, chosen, 0.0), CHOSEN, 1)
    around = side[...].astype(F32)
    xg[:, lat:] = (around + low).astype(BF16)
    differ = z[...] - target[...]
    consistency = jnp.mean(differ * differ, axis=-1, keepdims=True)
    rowloss[...] = column(around, WEIGHT) * (20.0 * consistency + 0.1 * log_prob)


def unit_kernel(
    total_rows, bins, flags, x, w1, w2, w3, vec,
    dx, h1_out, h2_out, dp1_out, dp2_out, dl_out, vgrad, n1, s1, n2, s2,
):
    @pl.when(pl.program_id(0) == 0)
    def _():
        vgrad[...] = jnp.zeros_like(vgrad)

    ce, probe, value = flags[0], flags[1], flags[2]
    b1, g1, b2, g2 = (vec[i : i + 1, :] for i in range(4))
    h, normed, slope, scale1 = norm_mish(dot(x[...], w1[...]) + b1, g1)
    n1[...] = normed
    s1[...] = slope
    h1 = h.astype(BF16)
    h1_out[...] = h1
    h, normed, slope, scale2 = norm_mish(dot(h1, w2[...]) + b2, g2)
    n2[...] = normed
    s2[...] = slope
    h2 = h.astype(BF16)
    h2_out[...] = h2
    logits = dot(h2, w3[...]) + vec[4:5, :128]
    lane = lanes(logits.shape)
    valid = lane < bins
    side = x[:, WIDTH - 128 :].astype(F32)
    label = jnp.where(value > 0.5, column(side, VBIN), column(side, RBIN))
    weight = column(side, WEIGHT)
    hot = jnp.where(lane.astype(F32) == label, 1.0, 0.0)
    top = jnp.max(jnp.where(valid, logits, -jnp.inf), axis=-1, keepdims=True)
    e = jnp.where(valid, jnp.exp(logits - top), 0.0)
    total = jnp.sum(e, axis=-1, keepdims=True)
    p = e / total
    centers = -10.0 + 20.0 * lane.astype(F32) / (bins - 1)
    estimate = jnp.sum(p * centers, axis=-1, keepdims=True)
    entropy = top + jnp.log(total) - jnp.sum(hot * logits, axis=-1, keepdims=True)
    loss = weight * (ce * entropy - probe * estimate)
    dl = (weight / total_rows) * (ce * (p - hot) - probe * p * (centers - estimate))
    low = dl.astype(BF16)
    dl_out[...] = low
    vgrad[4:5, :128] += jnp.sum(dl, axis=0, keepdims=True)
    dp2, gg, bg = norm_mish_back(dot_nt(low, w3[...]), n2[...], s2[...], scale2, g2)
    vgrad[2:3, :] += bg
    vgrad[3:4, :] += gg
    low = dp2.astype(BF16)
    dp2_out[...] = low
    dp1, gg, bg = norm_mish_back(dot_nt(low, w2[...]), n1[...], s1[...], scale1, g1)
    vgrad[0:1, :] += bg
    vgrad[1:2, :] += gg
    low = dp1.astype(BF16)
    dp1_out[...] = low
    grad = dot_nt(low, w1[...])
    lat = WIDTH - 128
    dx[:, :lat] = jnp.where(probe > 0.0, 0.0, grad[:, :lat]).astype(BF16)
    high = loss.astype(BF16).astype(F32)
    lane = lanes((grad.shape[0], 128))
    tail = jnp.where(lane == RBIN, high, jnp.where(lane == VBIN, loss - high, grad[:, lat:]))
    dx[:, lat:] = tail.astype(BF16)


def policy_back_kernel(
    total_rows, dxs, side, noise, pout, vec, p1, p2, p3, n1, s1, r1, n2, s2, r2,
    dp1_out, dp2_out, do_out, demb, vgrad,
):
    def v(name, width=1024):
        return vec[VEC[name] : VEC[name] + 1, :width]

    raw = pout[:, 128:]
    eps = noise[...]
    valid = lanes(raw.shape) < 8
    bent = jnp.tanh(raw)
    spread = jnp.exp(-10.0 + 6.0 * (bent + 1.0))
    chosen = jnp.tanh(pout[:, :128] + spread * eps)
    dchosen = pltpu.roll(dxs[...], 128 - CHOSEN, 1)
    g = column(side[...].astype(F32), WEIGHT) * (0.1 / total_rows)
    dmoved = jnp.where(valid, dchosen * (1.0 - chosen * chosen) + 2.0 * g * chosen, 0.0)
    draw = jnp.where(valid, (dmoved * spread * eps - g) * 6.0 * (1.0 - bent * bent), 0.0)
    do = jnp.concatenate([dmoved, draw], axis=1)
    low = do.astype(BF16)
    do_out[...] = low
    vgrad[...] = jnp.zeros_like(vgrad)
    vgrad[4:5, :256] = jnp.sum(do, axis=0, keepdims=True)
    dp2, gg, bg = norm_mish_back(dot_nt(low, p3[...]), n2[...], s2[...], r2[...], v("pg2"))
    vgrad[2:3, :] = bg
    vgrad[3:4, :] = gg
    low = dp2.astype(BF16)
    dp2_out[...] = low
    dp1, gg, bg = norm_mish_back(dot_nt(low, p2[...]), n1[...], s1[...], r1[...], v("pg1"))
    vgrad[0:1, :] = bg
    vgrad[1:2, :] = gg
    low = dp1.astype(BF16)
    dp1_out[...] = low
    demb[...] = dot_nt(low, p1[WIDTH - 128 :, :])


def chain_back_kernel(
    steps, total_rows, dxs, side, target, z0, z, vec, e1, e2, d1, d2, d3,
    e_n, e_s, e_r, d_n1, d_s1, d_r1, d_n2, d_s2, d_r2,
    d_p1, d_p2, d_p3, e_p1, e_p2, demb, obs_grad, vgrad,
):
    rows, lat = z0.shape

    def v(name, width=1024):
        return vec[VEC[name] : VEC[name] + 1, :width]

    vgrad[...] = jnp.zeros_like(vgrad)
    carried = jnp.zeros((rows, lat), F32)
    for t in range(steps - 1, -1, -1):
        at = slice(t * rows, (t + 1) * rows)
        here = z[at, :]
        weight = column(side[at, :].astype(F32), WEIGHT)
        up = carried + (weight * (40.0 / lat / total_rows)) * (here - target[at, :])
        dp3 = by_block(simnorm_back_block, here, up)
        vgrad[7:8, :lat] += jnp.sum(dp3, axis=0, keepdims=True)
        low = dp3.astype(BF16)
        d_p3[at, :] = low
        dp2, gg, bg = norm_mish_back(
            dot_nt(low, d3[...]), d_n2[at, :], d_s2[at, :], d_r2[at, :], v("dg2")
        )
        vgrad[5:6, :] += bg
        vgrad[6:7, :] += gg
        low = dp2.astype(BF16)
        d_p2[at, :] = low
        dp1, gg, bg = norm_mish_back(
            dot_nt(low, d2[...]), d_n1[at, :], d_s1[at, :], d_r1[at, :], v("dg1")
        )
        vgrad[3:4, :] += bg
        vgrad[4:5, :] += gg
        low = dp1.astype(BF16)
        d_p1[at, :] = low
        joined = dot_nt(low, d1[...]) + dxs[at, :]
        carried = joined[:, :lat]
        demb[at, :] = joined[:, lat:]
    dp2 = by_block(simnorm_back_block, z0[...], carried)
    vgrad[2:3, :lat] = jnp.sum(dp2, axis=0, keepdims=True)
    low = dp2.astype(BF16)
    e_p2[...] = low
    dp1, gg, bg = norm_mish_back(dot_nt(low, e2[...]), e_n[...], e_s[...], e_r[...], v("eg1"))
    vgrad[0:1, :] = bg
    vgrad[1:2, :] = gg
    low = dp1.astype(BF16)
    e_p1[...] = low
    obs_grad[...] = dot_nt(low, e1[...]) * total_rows


def shape(dims, dtype):
    return jax.ShapeDtypeStruct(dims, dtype)


def whole_call(kernel, out_shape, flops, *args):
    spec = pl.BlockSpec(memory_space=VMEM)
    moved = sum(math.prod(a.shape) * a.dtype.itemsize for a in tuple(args) + tuple(out_shape))
    return pl.pallas_call(
        kernel,
        out_shape=out_shape,
        in_specs=[spec] * len(args),
        out_specs=[spec] * len(out_shape),
        compiler_params=pltpu.CompilerParams(vmem_limit_bytes=56 * 1024 * 1024),
        cost_estimate=pl.CostEstimate(flops=flops, bytes_accessed=moved, transcendentals=0),
    )(*args)


def swap(array, axis, size, bit):
    return lax.ppermute(array, axis, [(i, i ^ bit) for i in range(size)])


def shift(array, axis, size, by):
    return lax.ppermute(array, axis, [(i, i + by) for i in range(size) if 0 <= i + by < size])


def own(stack, at):
    return lax.dynamic_index_in_dim(stack, at, 0, keepdims=False)


def gather_narrow(array, count):
    if count != 4:
        return lax.all_gather(array, "narrow", axis=0)
    half = array.shape[0] // 2
    one = swap(array, "narrow", 4, 1)
    two = swap(array, "narrow", 4, 2)
    three = jnp.concatenate(
        [swap(one[:half], "narrow", 4, 2), swap(two[half:], "narrow", 4, 1)], axis=0
    )
    me = lax.axis_index("narrow")
    near = [array, one, two, three]
    return jnp.stack([own(jnp.stack(near), me ^ k) for k in range(4)])


def gather_shared(array, count, wide):
    if count != 4:
        return gather_narrow(array, count)
    half = array.shape[0] // 2
    core = lax.axis_index("wide") % 2
    mine = gather_narrow(lax.dynamic_slice_in_dim(array, core * half, half, 0), count)
    other = swap(mine, "wide", wide, 1)
    return jnp.concatenate(
        [jnp.where(core == 0, mine, other), jnp.where(core == 0, other, mine)], axis=1
    )


def slot_groups(wide):
    return [list(range(i, i + SLOTS)) for i in range(0, wide, SLOTS)]


def gather_slots(array, wide):
    if wide != SLOTS:
        return lax.all_gather(array, "wide", axis=0, axis_index_groups=slot_groups(wide))
    z = lax.axis_index("wide") // 2
    core = lax.axis_index("wide") % 2
    line = [shift(array, "wide", wide, 2 * k) for k in (3, 2, 1)]
    line = line + [array] + [shift(array, "wide", wide, -2 * k) for k in (1, 2, 3)]
    mine = lax.dynamic_slice_in_dim(jnp.stack(line), 3 - z, 4, 0)
    other = swap(mine, "wide", wide, 1)
    both = jnp.stack(
        [jnp.where(core == 0, mine, other), jnp.where(core == 0, other, mine)], axis=1
    )
    return both.reshape((SLOTS,) + array.shape)


def sum_slots(array, wide):
    if wide != SLOTS:
        pieces = lax.all_to_all(array, "wide", 0, 0, axis_index_groups=slot_groups(wide))
        return jnp.sum(pieces.astype(F32), axis=0)
    z = lax.axis_index("wide") // 2
    core = lax.axis_index("wide") % 2
    pairs = array.reshape((4, 2) + array.shape[1:])
    mine = lax.dynamic_index_in_dim(pairs, core, 1, keepdims=False)
    away = lax.dynamic_index_in_dim(pairs, 1 - core, 1, keepdims=False)
    mine = (mine.astype(F32) + swap(away, "wide", wide, 1).astype(F32)).astype(BF16)
    total = own(mine, z).astype(F32)
    for k in (1, 2, 3):
        for by in (k, -k):
            to = jnp.clip(z + by, 0, 3)
            total = total + shift(own(mine, to), "wide", wide, 2 * by).astype(F32)
    return total


def pad_to(array, rows, columns):
    return jnp.pad(array, ((0, rows - array.shape[0]), (0, columns - array.shape[1])))


def on_device(
    wide, narrow, obs, actions, target_latents, noise, horizon, step_mask, task_ids, reward_bins, value_bins,
    task_table, encoder_first, encoder_second, dynamics_first, dynamics_second, dynamics_third,
    reward_first, reward_second, reward_third, critic_first, critic_second, critic_third,
    policy_first, policy_second, policy_third, encoder_bias, encoder_gain, dynamics_bias, dynamics_gain,
    reward_bias, reward_gain, critic_bias, critic_gain, policy_bias, policy_gain,
):
    rows, steps, act = actions.shape
    tall = rows * steps
    total_rows = rows * wide * narrow
    lat = encoder_second.shape[1]
    feat = encoder_first.shape[1]
    tasks, emb = task_table.shape
    bins = reward_third.shape[-1]
    heads = critic_first.shape[0]
    first = encoder_first.shape[0]
    joint = dynamics_first.shape[0]
    plain = policy_first.shape[0]
    deep = encoder_second.shape[0]
    slot = lax.axis_index("wide") % SLOTS
    head = jnp.asarray(SLOT_HEAD, jnp.int32)[slot]
    is_probe = jnp.asarray(SLOT_PROBE, jnp.int32)[slot] == 1
    is_reward = jnp.asarray(SLOT_REWARD, jnp.int32)[slot] == 1

    base = jnp.concatenate(
        [
            dynamics_second,
            encoder_second,
            dynamics_third,
            pad_to(jnp.concatenate([encoder_first, dynamics_first], axis=0), deep, feat),
        ],
        axis=1,
    )
    base = gather_shared(base, narrow, wide)
    acting = jnp.concatenate(
        [policy_second, pad_to(policy_third, deep, 128), pad_to(policy_first, deep, feat)], axis=1
    )
    acting = gather_shared(acting, narrow, wide)

    def pick(values, reward):
        return jnp.where(is_reward, reward, own(values, head))

    unit = jnp.concatenate(
        [
            pick(critic_second, reward_second),
            pad_to(pick(critic_third, reward_third), deep, 128),
            pad_to(pick(critic_first, reward_first), deep, feat),
        ],
        axis=1,
    )
    unit = gather_narrow(unit, narrow)
    full = narrow * deep
    gap = jnp.zeros((act, feat), BF16)
    d2 = base[:, :, :feat].reshape(full, feat)
    e2 = base[:, :, feat : feat + lat].reshape(full, lat)
    d3 = base[:, :, feat + lat : feat + 2 * lat].reshape(full, lat)
    e1 = base[:, :first, feat + 2 * lat :].reshape(narrow * first, feat)
    d1 = base[:, first : first + joint, feat + 2 * lat :].reshape(narrow * joint, feat)
    d1 = pad_to(d1, WIDTH, feat)
    p2 = acting[:, :, :feat].reshape(full, feat)
    p3 = acting[:, :, feat : feat + 2 * act].reshape(full, 2 * act)
    p3 = jnp.concatenate([pad_to(p3[:, :act], full, 128), pad_to(p3[:, act:], full, 128)], axis=1)
    p1 = acting[:, :plain, feat + 128 :].reshape(narrow * plain, feat)
    p1 = pad_to(jnp.concatenate([p1[:lat], gap, p1[lat:]], axis=0), WIDTH, feat)
    w2 = unit[:, :, :feat].reshape(full, feat)
    w3 = unit[:, :, feat : feat + 128].reshape(full, 128)
    w1 = unit[:, :joint, feat + 128 :].reshape(narrow * joint, feat)
    moved = w1[lat : lat + act]
    w1 = jnp.concatenate(
        [
            w1[:lat],
            jnp.where(is_probe, 0, moved),
            w1[lat + act :],
            jnp.where(is_probe, moved, 0),
            jnp.zeros((WIDTH - lat - 2 * act - emb, feat), BF16),
        ],
        axis=0,
    )

    def line(vector, start, width):
        return jnp.pad(vector[start : start + width], (0, feat - width))

    third = jnp.zeros((128 - act,), F32)
    vec = jnp.stack(
        [
            line(encoder_bias, 0, feat),
            encoder_gain,
            line(encoder_bias, feat, lat),
            line(dynamics_bias, 0, feat),
            line(dynamics_gain, 0, feat),
            line(dynamics_bias, feat, feat),
            line(dynamics_gain, feat, feat),
            line(dynamics_bias, 2 * feat, lat),
            line(policy_bias, 0, feat),
            line(policy_gain, 0, feat),
            line(policy_bias, feat, feat),
            line(policy_gain, feat, feat),
            jnp.concatenate(
                [
                    policy_bias[2 * feat : 2 * feat + act],
                    third,
                    policy_bias[2 * feat + act :],
                    jnp.zeros((feat - 128 - act,), F32),
                ]
            ),
        ]
        + [jnp.zeros((feat,), F32)] * 3
    )
    unit_bias = pick(critic_bias, reward_bias)
    unit_gain = pick(critic_gain, reward_gain)
    unit_vec = jnp.stack(
        [
            line(unit_bias, 0, feat),
            line(unit_gain, 0, feat),
            line(unit_bias, feat, feat),
            line(unit_gain, feat, feat),
            line(unit_bias, 2 * feat, bins),
        ]
        + [jnp.zeros((feat,), F32)] * 3
    )

    def by_step(array):
        return jnp.swapaxes(array, 0, 1).reshape((tall,) + array.shape[2:])

    onehot = (task_ids[:, None] == jnp.arange(tasks, dtype=jnp.int32)[None, :]).astype(F32)
    embed = jnp.dot(onehot, task_table, precision=lax.Precision.HIGHEST).astype(BF16)
    moment = jnp.arange(steps, dtype=jnp.int32)[None, :]
    weighting = (
        jnp.where(moment < horizon[:, None], 1.0, 0.0)
        * step_mask.astype(F32)
        * (0.5 ** moment.astype(F32))
    )
    side = jnp.concatenate(
        [
            by_step(actions).astype(BF16),
            jnp.tile(embed, (steps, 1)),
            jnp.zeros((tall, RBIN - act - emb), BF16),
            by_step(reward_bins)[:, None].astype(BF16),
            by_step(value_bins)[:, None].astype(BF16),
            by_step(weighting)[:, None].astype(BF16),
            jnp.zeros((tall, 127 - WEIGHT), BF16),
        ],
        axis=1,
    )
    eps = pad_to(by_step(noise), tall, 128)
    target = by_step(target_latents)

    wide_f = shape((tall, feat), F32)
    wide_b = shape((tall, feat), BF16)
    one = shape((tall, 1), F32)
    kept = [wide_b, wide_f, wide_f, one]
    (
        xg, z0, z, rowloss, e_h, e_n, e_s, e_r, d_h1, d_n1, d_s1, d_r1, d_h2, d_n2, d_s2, d_r2,
        p_h1, p_n1, p_s1, p_r1, p_h2, p_n2, p_s2, p_r2, pout,
    ) = whole_call(
        functools.partial(forward_kernel, steps),
        [
            shape((tall, WIDTH), BF16), shape((rows, lat), F32), shape((tall, lat), F32), one,
            shape((rows, feat), BF16), shape((rows, feat), F32), shape((rows, feat), F32), shape((rows, 1), F32),
        ] + kept * 4 + [shape((tall, 256), F32)],
        2 * tall * 5 * feat * feat,
        obs, side, eps, target, vec, e1, e2, d1, d2, d3, p1, p2, p3,
    )

    x = gather_slots(xg, wide).reshape(SLOTS * tall, WIDTH)
    ce = jnp.where(is_reward, 0.1, jnp.where(is_probe, 0.0, 0.1 / heads))
    flags = jnp.stack([ce, jnp.where(is_probe, 0.5, 0.0), jnp.where(is_reward, 0.0, 1.0)])
    dx, h1, h2, dp1, dp2, dl, unit_vgrad = run_unit(
        flags.astype(F32), x, w1, w2, w3, unit_vec, tall, total_rows, bins
    )
    dxs = sum_slots(dx.reshape(SLOTS, tall, WIDTH), wide)
    rowloss = rowloss[:, 0] + dxs[:, lat + RBIN] + dxs[:, lat + VBIN]
    row_loss = jnp.sum(rowloss.reshape(steps, rows), axis=0)

    side_f = dxs[:, lat:]
    pp1, pp2, po, pemb, p_vgrad = whole_call(
        functools.partial(policy_back_kernel, total_rows),
        [wide_b, wide_b, shape((tall, 256), BF16), shape((tall, 128), F32), shape((8, feat), F32)],
        2 * tall * 2 * feat * feat,
        side_f, side, eps, pout, vec, p1, p2, p3, p_n1, p_s1, p_r1, p_n2, p_s2, p_r2,
    )
    cp1, cp2, cp3, ep1, ep2, cemb, obs_grad, c_vgrad = whole_call(
        functools.partial(chain_back_kernel, steps, total_rows),
        [
            wide_b, wide_b, shape((tall, lat), BF16), shape((rows, feat), BF16), shape((rows, lat), BF16),
            shape((tall, 128), F32), shape(obs.shape, F32), shape((8, feat), F32),
        ],
        2 * tall * 3 * feat * feat,
        dxs, side, target, z0, z, vec, e1, e2, d1, d2, d3,
        e_n, e_s, e_r, d_n1, d_s1, d_r1, d_n2, d_s2, d_r2,
    )
    embed_grad = jnp.sum((pemb + cemb)[:, act : act + emb].reshape(steps, rows, emb), axis=0)
    table_grad = jnp.einsum("rt,rd->td", onehot, embed_grad, precision=lax.Precision.HIGHEST)

    def low(a, b):
        return dot_tn(a, b).astype(BF16)

    def spread(grad, per):
        return jnp.pad(grad.reshape(narrow, per, feat), ((0, 0), (0, deep - per), (0, 0)))

    g_unit1 = low(x, dp1)[:joint * narrow].reshape(narrow, joint, feat)
    g_unit = jnp.concatenate(
        [
            low(h1, dp2).reshape(narrow, deep, feat),
            low(h2, dl).reshape(narrow, deep, 128),
            jnp.pad(g_unit1, ((0, 0), (0, deep - joint), (0, 0))),
        ],
        axis=2,
    )
    g_act1 = low(xg, pp1)
    g_act1 = jnp.concatenate([g_act1[:lat], g_act1[lat + act : lat + act + emb]], axis=0)
    g_act3 = low(p_h2, po)
    g_act3 = jnp.concatenate([g_act3[:, :act], g_act3[:, 128 : 128 + act]], axis=1)
    g_act = jnp.concatenate(
        [
            low(p_h1, pp2).reshape(narrow, deep, feat),
            pad_to(g_act3, full, 128).reshape(narrow, deep, 128),
            spread(g_act1, plain),
        ],
        axis=2,
    )
    g_e1 = low(obs, ep1).reshape(narrow, first, feat)
    g_d1 = low(xg, cp1)[: joint * narrow].reshape(narrow, joint, feat)
    g_base = jnp.concatenate(
        [
            low(d_h1, cp2).reshape(narrow, deep, feat),
            low(e_h, ep2).reshape(narrow, deep, lat),
            low(d_h2, cp3).reshape(narrow, deep, lat),
            jnp.pad(
                jnp.concatenate([g_e1, g_d1], axis=1),
                ((0, 0), (0, deep - first - joint), (0, 0)),
            ),
        ],
        axis=2,
    )

    def scatter(array):
        return lax.psum_scatter(array, "narrow", scatter_dimension=0, tiled=False)

    g_unit = scatter(g_unit)
    if wide != SLOTS:
        same = [list(range(i, wide, SLOTS)) for i in range(SLOTS)]
        g_unit = lax.psum(g_unit, "wide", axis_index_groups=same)
    g_unit = lax.all_gather(
        g_unit, "wide", axis=0, axis_index_groups=None if wide == SLOTS else slot_groups(wide)
    )
    g_act = lax.psum(scatter(g_act), "wide")
    g_base = lax.psum(scatter(g_base), "wide")
    slots = jnp.where(jnp.arange(SLOTS)[:, None, None] == slot, unit_vgrad[None, :5], 0.0)
    small = jnp.concatenate([slots.reshape(-1), p_vgrad[:5].reshape(-1), c_vgrad.reshape(-1), table_grad.reshape(-1)])
    small = lax.psum(small, ("wide", "narrow"))
    s_unit = small[: SLOTS * 5 * feat].reshape(SLOTS, 5, feat)
    small = small[SLOTS * 5 * feat :]
    s_pol = small[: 5 * feat].reshape(5, feat)
    s_chain = small[5 * feat : 13 * feat].reshape(8, feat)
    grad_table = small[13 * feat :].reshape(tasks, emb)

    g_unit = g_unit.astype(F32)
    g_act = g_act.astype(F32)
    g_base = g_base.astype(F32)
    pick_heads = [g_unit[s] for s in HEAD_SLOT]
    reward = g_unit[REWARD_SLOT]

    def first_of(a):
        return a[:joint, feat + 128 :]

    def second_of(a):
        return a[:, :feat]

    def third_of(a):
        return a[:, feat : feat + bins]

    def biases(s):
        return jnp.concatenate([s[0], s[2], s[4, :bins]])

    def gains(s):
        return jnp.concatenate([s[1], s[3]])

    return (
        row_loss,
        jnp.swapaxes(z.reshape(steps, rows, lat), 0, 1),
        obs_grad,
        grad_table,
        g_base[:first, feat + 2 * lat :],
        g_base[:, feat : feat + lat],
        g_base[first : first + joint, feat + 2 * lat :],
        g_base[:, :feat],
        g_base[:, feat + lat : feat + 2 * lat],
        first_of(reward),
        second_of(reward),
        third_of(reward),
        jnp.stack([first_of(a) for a in pick_heads]),
        jnp.stack([second_of(a) for a in pick_heads]),
        jnp.stack([third_of(a) for a in pick_heads]),
        g_act[:plain, feat + 128 :],
        g_act[:, :feat],
        g_act[:, feat : feat + 2 * act],
        jnp.concatenate([s_chain[0], s_chain[2, :lat]]),
        s_chain[1],
        jnp.concatenate([s_chain[3], s_chain[5], s_chain[7, :lat]]),
        jnp.concatenate([s_chain[4], s_chain[6]]),
        biases(s_unit[REWARD_SLOT]),
        gains(s_unit[REWARD_SLOT]),
        jnp.stack([biases(s_unit[s]) for s in HEAD_SLOT]),
        jnp.stack([gains(s_unit[s]) for s in HEAD_SLOT]),
        jnp.concatenate([s_pol[0], s_pol[2], s_pol[4, :act], s_pol[4, 128 : 128 + act]]),
        jnp.concatenate([s_pol[1], s_pol[3]]),
    )


def run_unit(flags, x, w1, w2, w3, vec, tile, total_rows, bins):
    tall = x.shape[0]
    feat = w2.shape[0]

    def rowed(width):
        return pl.BlockSpec((tile, width), lambda i: (i, 0))

    def fixed(array):
        return pl.BlockSpec(array.shape, lambda i: (0, 0), pipeline_mode=pl.Buffered(1))

    scratch = pltpu.VMEM((tile, feat), F32)
    return pl.pallas_call(
        functools.partial(unit_kernel, total_rows, bins),
        grid=(tall // tile,),
        in_specs=[
            pl.BlockSpec(memory_space=pltpu.MemorySpace.SMEM),
            rowed(WIDTH),
            fixed(w1),
            fixed(w2),
            fixed(w3),
            fixed(vec),
        ],
        out_specs=[
            rowed(WIDTH),
            rowed(feat),
            rowed(feat),
            rowed(feat),
            rowed(feat),
            rowed(128),
            pl.BlockSpec((8, feat), lambda i: (0, 0)),
        ],
        out_shape=[
            shape((tall, WIDTH), BF16),
            shape((tall, feat), BF16),
            shape((tall, feat), BF16),
            shape((tall, feat), BF16),
            shape((tall, feat), BF16),
            shape((tall, 128), BF16),
            shape((8, feat), F32),
        ],
        scratch_shapes=[scratch] * 4,
        compiler_params=pltpu.CompilerParams(vmem_limit_bytes=56 * 1024 * 1024),
        cost_estimate=pl.CostEstimate(
            flops=8 * tall * feat * feat, bytes_accessed=tall * feat * 12, transcendentals=0
        ),
    )(flags, x, w1, w2, w3, vec)


def solution(mesh):
    both = P(("wide", "narrow"))
    by_row = P("narrow")
    by_head = P(None, "narrow")
    matrices = (by_row,) * 8 + (by_head,) * 3 + (by_row,) * 3
    return jax.shard_map(
        functools.partial(on_device, mesh.shape["wide"], mesh.shape["narrow"]),
        mesh=mesh,
        in_specs=(both,) * 9 + (P(),) + matrices + (P(),) * 10,
        out_specs=(both,) * 3 + (P(),) + matrices + (P(),) * 10,
        check_vma=False,
    )
```

profile of v0, /device:TPU:0, one launch (start us, length us, event | category | flops | bytes accessed | tf_op | source)
XLA Modules:
  0.0 803.4 jit_solution(12815090913022476201)
XLA Ops:
  54.5 20.9 %collective-permute-done.8 = bf16[64,2176]{1,0:T(8,128)(2,1)} collective-permute-done((bf16[64,2176]{1,0:T(8,128)(2,1)}, bf16[64,2176]{1,0:T(8,128)(2,1)}, u32[]{:S(2)}, u32[]{:S(2)}) %collective-permute-start.8) | collective-permute-done | bytes 278560 | tf_op jit(solution)/shard_map/ppermute | solution.py:319
  84.4 5.4 collective-permute-done.2
  104.8 8.2 %collective-permute-done.19 = bf16[128,2176]{1,0:T(8,128)(2,1)} collective-permute-done((bf16[128,2176]{1,0:T(8,128)(2,1)}, bf16[128,2176]{1,0:T(8,128)(2,1)}, u32[]{:S(2)}, u32[]{:S(2)}) %collective-permute-start.19) | collective-permute-done | bytes 557088 | tf_op jit(solution)/shard_map/ppermute | solution.py:319
  138.4 23.3 %shard_map.564 = (bf16[240,896]{1,0:T(8,128)(2,1)}, f32[48,768]{1,0:T(8,128)}, f32[240,768]{1,0:T(8,128)}, f32[240,1]{1,0:T(8,128)}, bf16[48,1024]{1,0:T(8,128)(...) custom-call(bf16[48,128]{1,0:T(8,128)(2,1)} %obs.1, ...), custom_call_target="tpu_custom_call" | custom-call | flops 2516582400 | bytes 24683392 | tf_op jit(solution)/shard_map/pallas_call | solution.py:308
  161.7 5.6 collective-permute-start.10
  179.4 7.9 collective-permute-done.11
  187.3 7.4 collective-permute-done.12
  194.9 16.9 %collective-permute-done.14 = bf16[240,896]{1,0:T(8,128)(2,1)S(1)} collective-permute-done((bf16[240,896]{1,0:T(8,128)(2,1)S(1)}, bf16[240,896]{1,0:T(8,128)(2,1)S(1)}, u32[]{:S(2)}, u32[]{:S(2)}) %collective-permute-start.14) | collective-permute-done | bytes 430112 | tf_op jit(solution)/shard_map/ppermute | solution.py:323
  232.1 42.1 %shard_map.565 = (bf16[1920,896]{1,0:T(8,128)(2,1)}, bf16[1920,1024]{1,0:T(8,128)(2,1)}, bf16[1920,1024]{1,0:T(8,128)(2,1)}, bf16[1920,1024]{1,0:T(8,128)(2,1)},...) custom-call(f32[3]{0:T(128)} %pad_maximum_fusion.33.flags, bf16[1920,896]{1,0:T(8,128)(2,1)} %bitcast.275, ...), custom_call_target="tpu_custom_call" | custom-call | flops 16106127360 | bytes 23592960 | tf_op jit(solution)/shard_map/pallas_call | solution.py:718
  285.4 4.7 collective-permute-start.24
  291.4 5.7 collective-permute-start.26
  298.6 5.0 collective-permute-done.24
  303.6 22.0 %collective-permute-done.25 = bf16[240,896]{1,0:T(8,128)(2,1)S(1)} collective-permute-done((bf16[240,896]{1,0:T(8,128)(2,1)}, bf16[240,896]{1,0:T(8,128)(2,1)S(1)}, u32[]{:S(2)}, u32[]{:S(2)}) %collective-permute-start.25) | collective-permute-done | bytes 430112 | tf_op jit(solution)/shard_map/ppermute | solution.py:323
  329.1 6.4 shard_map.567
  354.4 18.4 %shard_map.566 = (bf16[240,1024]{1,0:T(8,128)(2,1)}, bf16[240,1024]{1,0:T(8,128)(2,1)}, bf16[240,768]{1,0:T(8,128)(2,1)}, bf16[48,1024]{1,0:T(8,128)(2,1)}, bf16...) custom-call(f32[240,896]{1,0:T(8,128)} %copy-done.10, ...), custom_call_target="tpu_custom_call" | custom-call | flops 1509949440 | bytes 15980608 | tf_op jit(solution)/shard_map/pallas_call | solution.py:308
  386.4 6.2 fusion.76
  399.6 6.9 convolution_convert_fusion.1
  411.2 78.7 %reduce-scatter.10.cloned.1.call-done = bf16[1,256,3584]{2,1,0:T(8,128)(2,1)} async-done(((bf16[4,256,3584]{2,1,0:T(8,128)(2,1)}), bf16[1,256,3584]{2,1,0:T(8,128)(2,1)}) %reduce-scatter.10.cloned.1.call-update) | async-done | bytes 1835024
  490.2 58.6 %reduce-scatter.12.cloned.1.call-done = bf16[1,256,2176]{2,1,0:T(8,128)(2,1)} async-done(((bf16[4,256,2176]{2,1,0:T(8,128)(2,1)}), bf16[1,256,2176]{2,1,0:T(8,128)(2,1)}) %reduce-scatter.12.cloned.1.call-update) | async-done | bytes 1114128
  550.7 36.1 %all-reduce.24.cloned.1.call-done = f32[61952]{0:T(1024)} async-done(((f32[61952]{0:T(1024)}), f32[61952]{0:T(1024)}) %all-reduce.24.cloned.1.call-update) | async-done | bytes 247824 | tf_op jit(solution)/shard_map/psum | solution.py:647
  597.4 65.6 %all-reduce.26.cloned.1.call-done = (bf16[256,3584]{1,0:T(8,128)(2,1)}, bf16[256,2176]{0,1:T(8,128)(2,1)}) async-done(((bf16[256,3584]{1,0:T(8,128)(2,1)}, bf16[256,2176]{0,1:T(8,128)(2,1)}), (bf16[256,3584]{1,0:T(8,128)(2,1)}, bf16[256,2176]{0,1:T(8,128)(2,1)})) %all-reduce.26.cloned.1.call-update) | async-done | bytes 2949136 | tf_op jit(solution)/shard_map/psum | solution.py:644
  675.5 74.5 %all-gather.2.cloned.1.call-done = bf16[8,256,2176]{2,1,0:T(8,128)(2,1)} async-done(((bf16[1,256,2176]{2,1,0:T(8,128)(2,1)}), bf16[8,256,2176]{2,1,0:T(8,128)(2,1)}) %all-gather.2.cloned.1.call-update) | async-done | bytes 8912912 | tf_op jit(solution)/shard_map/all_gather | solution.py:640
  750.0 10.9 %convert_element_type.228 = f32[8,256,2176]{2,1,0:T(8,128)} convert(bf16[8,256,2176]{2,1,0:T(8,128)(2,1)} %all-gather.2.cloned.1.call-done) | non-fusion elementwise | flops 4456448 | bytes 26738688 | tf_op jit(solution)/shard_map/convert_element_type | solution.py:654
  760.9 9.1 %slice_bitcast_fusion = (f32[256,2176]{1,0:T(8,128)S(1)}, f32[256,2176]{1,0:T(8,128)}, f32[256,2176]{1,0:T(8,128)}, f32[256,2176]{1,0:T(8,128)}, f32[256,2176]{1,0:T(8,128)}, /*index=5*/f32[256,2176]{1,0:T(8,128)}) fusion(f32[8,256,2176]{2,1,0:T(8,128)} %convert_element_type.228), kind=kLoop, calls=%fused_computation.31 | loop fusion | bytes 26738688 | tf_op jit(solution)/shard_map/squeeze | solution.py:657
  (439 shorter events, 236.1 us)
Async XLA Ops:
  8.1 403.1 %reduce-scatter.14.cloned.1.call-start = ((), (), s32[]{:S(2)}) async-start(), calls=%async_computation.7 | async-start | bytes 5570560
  10.2 20.5 %collective-permute-start.5 = (bf16[128,2176]{1,0:T(8,128)(2,1)S(1)}, bf16[128,2176]{1,0:T(8,128)(2,1)}, u32[]{:S(2)}, u32[]{:S(2)}) collective-permute-start(bf16[128,2176]{1,0:T(8,128)(2,1)S(1)} %fusion.46), channel_id=1, source_target_pairs={{0,1},{1,0},{2,3},{3,2},{4,5},{5,4},{6,7},{7,6},{8,9},{9,8},{10,11... | collective-permute-start | bytes 1671176 | tf_op jit(solution)/shard_map/ppermute | solution.py:319
  13.2 20.7 %collective-permute-start.6 = (bf16[128,2176]{1,0:T(8,128)(2,1)S(1)}, bf16[128,2176]{1,0:T(8,128)(2,1)}, u32[]{:S(2)}, u32[]{:S(2)}) collective-permute-start(bf16[128,2176]{1,0:T(8,128)(2,1)S(1)} %fusion.46), channel_id=1, source_target_pairs={{0,2},{1,3},{2,0},{3,1},{4,6},{5,7},{6,4},{7,5},{8,10},{9,11},{10,... | collective-permute-start | bytes 1671176 | tf_op jit(solution)/shard_map/ppermute | solution.py:319
  15.9 62.2 %collective-permute-start = (bf16[128,3584]{1,0:T(8,128)(2,1)S(1)}, bf16[128,3584]{1,0:T(8,128)(2,1)S(1)}, u32[]{:S(2)}, u32[]{:S(2)}) collective-permute-start(bf16[128,3584]{1,0:T(8,128)(2,1)S(1)} %fusion.34), channel_id=1, source_target_pairs={{0,1},{1,0},{2,3},{3,2},{4,5},{5,4},{6,7},{7,6},{8,9},{9,8},{10,11... | collective-permute-start | bytes 2752520 | tf_op jit(solution)/shard_map/ppermute | solution.py:319
  16.5 63.4 %collective-permute-start.1 = (bf16[128,3584]{1,0:T(8,128)(2,1)S(1)}, bf16[128,3584]{1,0:T(8,128)(2,1)S(1)}, u32[]{:S(2)}, u32[]{:S(2)}) collective-permute-start(bf16[128,3584]{1,0:T(8,128)(2,1)S(1)} %fusion.34), channel_id=1, source_target_pairs={{0,2},{1,3},{2,0},{3,1},{4,6},{5,7},{6,4},{7,5},{8,10},{9,11},{10,... | collective-permute-start | bytes 2752520 | tf_op jit(solution)/shard_map/ppermute | solution.py:319
  25.0 70.7 %collective-permute-start.17 = (bf16[256,2176]{1,0:T(8,128)(2,1)}, bf16[256,2176]{1,0:T(8,128)(2,1)}, u32[]{:S(2)}, u32[]{:S(2)}) collective-permute-start(bf16[256,2176]{1,0:T(8,128)(2,1)} %fusion.19), channel_id=1, source_target_pairs={{0,1},{1,0},{2,3},{3,2},{4,5},{5,4},{6,7},{7,6},{8,9},{9,8},{10,11... | collective-permute-start | bytes 3342344 | tf_op jit(solution)/shard_map/ppermute | solution.py:319
  32.3 20.6 %collective-permute-start.7 = (bf16[64,2176]{1,0:T(8,128)(2,1)}, bf16[64,2176]{1,0:T(8,128)(2,1)}, u32[]{:S(2)}, u32[]{:S(2)}) collective-permute-start(bf16[64,2176]{1,0:T(8,128)(2,1)} %slice.650), channel_id=1, source_target_pairs={{0,2},{1,3},{2,0},{3,1},{4,6},{5,7},{6,4},{7,5},{8,10},{9,11},{10,... | collective-permute-start | bytes 835592 | tf_op jit(solution)/shard_map/ppermute | solution.py:319
  35.6 39.8 %collective-permute-start.8 = (bf16[64,2176]{1,0:T(8,128)(2,1)}, bf16[64,2176]{1,0:T(8,128)(2,1)}, u32[]{:S(2)}, u32[]{:S(2)}) collective-permute-start(bf16[64,2176]{1,0:T(8,128)(2,1)} %slice.651), channel_id=1, source_target_pairs={{0,1},{1,0},{2,3},{3,2},{4,5},{5,4},{6,7},{7,6},{8,9},{9,8},{10,11... | collective-permute-start | bytes 835592 | tf_op jit(solution)/shard_map/ppermute | solution.py:319
  53.0 45.3 %collective-permute-start.18 = (bf16[256,2176]{1,0:T(8,128)(2,1)}, bf16[256,2176]{1,0:T(8,128)(2,1)S(1)}, u32[]{:S(2)}, u32[]{:S(2)}) collective-permute-start(bf16[256,2176]{1,0:T(8,128)(2,1)} %fusion.19), channel_id=1, source_target_pairs={{0,2},{1,3},{2,0},{3,1},{4,6},{5,7},{6,4},{7,5},{8,10},{9,11},{10,... | collective-permute-start | bytes 3342344 | tf_op jit(solution)/shard_map/ppermute | solution.py:319
  84.4 35.7 %collective-permute-start.9 = (bf16[4,128,2176]{2,1,0:T(8,128)(2,1)}, bf16[4,128,2176]{2,1,0:T(8,128)(2,1)}, u32[]{:S(2)}, u32[]{:S(2)}) collective-permute-start(bf16[4,128,2176]{2,1,0:T(8,128)(2,1)} %pad_maximum_fusion.7), channel_id=1, source_target_pairs={{0,4},{4,0},{8,12},{12,8},{16,20},{20,16},{24,28},{28,24},{1,5},{5... | collective-permute-start | bytes 6684680 | tf_op jit(solution)/shard_map/ppermute | solution.py:319
  94.9 31.7 %collective-permute-start.4 = (bf16[4,128,3584]{2,1,0:T(8,128)(2,1)}, bf16[4,128,3584]{2,1,0:T(8,128)(2,1)}, u32[]{:S(2)}, u32[]{:S(2)}) collective-permute-start(bf16[4,128,3584]{2,1,0:T(8,128)(2,1)} %pad_maximum_fusion.4), channel_id=1, source_target_pairs={{0,4},{4,0},{8,12},{12,8},{16,20},{20,16},{24,28},{28,24},{1,5},{5... | collective-permute-start | bytes 11010056 | tf_op jit(solution)/shard_map/ppermute | solution.py:319
  167.3 19.9 %collective-permute-start.11 = (bf16[240,896]{1,0:T(8,128)(2,1)}, bf16[240,896]{1,0:T(8,128)(2,1)S(1)}, u32[]{:S(2)}, u32[]{:S(2)}) collective-permute-start(bf16[240,896]{1,0:T(8,128)(2,1)} %get-tuple-element.74), channel_id=1, source_target_pairs={{0,16},{4,20},{8,24},{12,28},{1,17},{5,21},{9,25},{13,29},{2,18},{... | collective-permute-start | bytes 1290248 | tf_op jit(solution)/shard_map/ppermute | solution.py:323
  169.5 25.3 %collective-permute-start.12 = (bf16[240,896]{1,0:T(8,128)(2,1)S(1)}, bf16[240,896]{1,0:T(8,128)(2,1)S(1)}, u32[]{:S(2)}, u32[]{:S(2)}) collective-permute-start(bf16[240,896]{1,0:T(8,128)(2,1)S(1)} %copy-done.21), channel_id=1, source_target_pairs={{0,8},{4,12},{8,16},{12,20},{16,24},{20,28},{1,9},{5,13},{9,17},{1... | collective-permute-start | bytes 1290248 | tf_op jit(solution)/shard_map/ppermute | solution.py:323
  171.9 22.9 %collective-permute-start.13 = (bf16[240,896]{1,0:T(8,128)(2,1)S(1)}, bf16[240,896]{1,0:T(8,128)(2,1)S(1)}, u32[]{:S(2)}, u32[]{:S(2)}) collective-permute-start(bf16[240,896]{1,0:T(8,128)(2,1)S(1)} %copy-done.21), channel_id=1, source_target_pairs={{8,0},{12,4},{16,8},{20,12},{24,16},{28,20},{9,1},{13,5},{17,9},{2... | collective-permute-start | bytes 1290248 | tf_op jit(solution)/shard_map/ppermute | solution.py:323
  173.2 38.6 %collective-permute-start.14 = (bf16[240,896]{1,0:T(8,128)(2,1)S(1)}, bf16[240,896]{1,0:T(8,128)(2,1)S(1)}, u32[]{:S(2)}, u32[]{:S(2)}) collective-permute-start(bf16[240,896]{1,0:T(8,128)(2,1)S(1)} %copy-done.21), channel_id=1, source_target_pairs={{16,0},{20,4},{24,8},{28,12},{17,1},{21,5},{25,9},{29,13},{18,2},{... | collective-permute-start | bytes 1290248 | tf_op jit(solution)/shard_map/ppermute | solution.py:323
  178.0 33.8 %collective-permute-start.15 = (bf16[240,896]{1,0:T(8,128)(2,1)S(1)}, bf16[240,896]{1,0:T(8,128)(2,1)S(1)}, u32[]{:S(2)}, u32[]{:S(2)}) collective-permute-start(bf16[240,896]{1,0:T(8,128)(2,1)S(1)} %copy-done.21), channel_id=1, source_target_pairs={{24,0},{28,4},{25,1},{29,5},{26,2},{30,6},{27,3},{31,7}} | collective-permute-start | bytes 1290248 | tf_op jit(solution)/shard_map/ppermute | solution.py:323
  290.1 35.5 %collective-permute-start.25 = (bf16[240,896]{1,0:T(8,128)(2,1)}, bf16[240,896]{1,0:T(8,128)(2,1)S(1)}, u32[]{:S(2)}, u32[]{:S(2)}) collective-permute-start(bf16[240,896]{1,0:T(8,128)(2,1)} %get-tuple-element.237), channel_id=1, source_target_pairs={{16,0},{20,4},{24,8},{28,12},{17,1},{21,5},{25,9},{29,13},{18,2},{... | collective-permute-start | bytes 1290248 | tf_op jit(solution)/shard_map/ppermute | solution.py:323
  291.4 34.2 %collective-permute-start.26 = (bf16[240,896]{1,0:T(8,128)(2,1)}, bf16[240,896]{1,0:T(8,128)(2,1)}, u32[]{:S(2)}, u32[]{:S(2)}) collective-permute-start(bf16[240,896]{1,0:T(8,128)(2,1)} %get-tuple-element.236), channel_id=1, source_target_pairs={{0,24},{4,28},{1,25},{5,29},{2,26},{6,30},{3,27},{7,31}} | collective-permute-start | bytes 1290248 | tf_op jit(solution)/shard_map/ppermute | solution.py:323
  297.1 29.3 %collective-permute-start.27 = (bf16[240,896]{1,0:T(8,128)(2,1)}, bf16[240,896]{1,0:T(8,128)(2,1)}, u32[]{:S(2)}, u32[]{:S(2)}) collective-permute-start(bf16[240,896]{1,0:T(8,128)(2,1)} %get-tuple-element.235), channel_id=1, source_target_pairs={{24,0},{28,4},{25,1},{29,5},{26,2},{30,6},{27,3},{31,7}} | collective-permute-start | bytes 1290248 | tf_op jit(solution)/shard_map/ppermute | solution.py:323
  354.2 135.7 %reduce-scatter.10.cloned.1.call-start = ((), (), s32[]{:S(2)}) async-start(), calls=%async_computation.5 | async-start | bytes 9175040
  384.4 164.4 %reduce-scatter.12.cloned.1.call-start = ((), (), s32[]{:S(2)}) async-start(), calls=%async_computation.6 | async-start | bytes 5570560
  408.9 178.0 %all-reduce.24.cloned.1.call-start = ((), (), s32[]{:S(2)}) async-start(), calls=%async_computation.3 | async-start | bytes 499712 | tf_op jit(solution)/shard_map/psum | solution.py:647
  411.1 251.9 %all-reduce.26.cloned.1.call-start = ((), (), s32[]{:S(2)}) async-start(), calls=%async_computation.8 | async-start | bytes 5898240 | tf_op jit(solution)/shard_map/psum | solution.py:644
  489.9 260.1 %all-gather.2.cloned.1.call-start = ((), (), s32[]{:S(2)}) async-start(), calls=%async_computation.4 | async-start | bytes 10027008 | tf_op jit(solution)/shard_map/all_gather | solution.py:640
  (91 other events, 825.8 us)
Sparse Core Ops, SparseCore 0:
  354.3 53.0 reduce-scatter.13
  410.5 79.3 reduce-scatter.9
  493.8 54.9 reduce-scatter.11
Sparse Core Ops, SparseCore 1:
  415.4 171.3 all-reduce.23
  589.2 73.8 all-reduce.25
  664.6 85.4 all-gather.1
where the time goes:
time: 812 us; the launch traced here: 803 us
  waiting for transfers between devices  420 us (52%)
  local copies, waits for them, and re-layouts  130 us (16%)
  Pallas kernels  90.2 us (11%)
  other arithmetic  70.6 us (9%)
  starting transfers between devices  46.2 us (6%)
  matrix products  25.8 us (3%)
  between operations  20.7 us (3%)
    unnamed x9, waiting for transfers between devices  137 us
    all_gather x1, waiting for transfers between devices, on_device(): lax.all_gather(g_unit, 'wide', axis=0, axis_index_groups=None if wide ==...  74.5 us
    psum x1, waiting for transfers between devices, on_device(): g_base = lax.psum(scatter(g_base), 'wide')  65.6 us
    ppermute x12, waiting for transfers between devices, shift(): lax.ppermute(array, axis, [(i, i + by) for i in range(size) if 0 <= i + b...  63 us
    pallas_call x3, Pallas kernels, whole_call(): pl.pallas_call(kernel, out_shape=out_shape, in_specs=[spec] * len(args),...  48.1 us
    ppermute x16, waiting for transfers between devices, swap(): return lax.ppermute(array, axis, [(i, i ^ bit) for i in range(size)])  43.6 us
    pallas_call x1, Pallas kernels, run_unit(): pl.pallas_call(functools.partial(unit_kernel, total_rows, bins), grid=(ta...  42.1 us
    unnamed x179, local copies, waits for them, and re-layouts  39.4 us
  transfers between devices with their start and end apart: 34, of which 19 were waited for; matrix products, arithmetic and copies ran while one was open for 16% of the time, Pallas kernels for 2%

commit v1 on v0

v1 whole, which is shorter than its diff:
```python
import functools
import math

import jax
import jax.numpy as jnp
from jax import lax
from jax.experimental import pallas as pl
from jax.experimental.pallas import tpu as pltpu
from jax.sharding import PartitionSpec as P

F32 = jnp.float32
BF16 = jnp.bfloat16
SLOTS = 8
SLOT_HEAD = (0, 1, 0, 1, 2, 3, 4, 0)
SLOT_PROBE = (0, 0, 1, 1, 0, 0, 0, 0)
SLOT_REWARD = (0, 0, 0, 0, 0, 0, 0, 1)
HEAD_SLOT = (0, 1, 4, 5, 6)
REWARD_SLOT = 7
MIB = 1024 * 1024
VMEM = pl.BlockSpec(memory_space=pltpu.MemorySpace.VMEM)
SMEM = pl.BlockSpec(memory_space=pltpu.MemorySpace.SMEM)
ANY = pl.BlockSpec(memory_space=pl.ANY)


def shape(dims, dtype):
    return jax.ShapeDtypeStruct(tuple(dims), dtype)


def call(kernel, out_shape, vmem=(), smem=(), hbm=(), token=(), scratch=(), flops=0, limit=48):
    given = len(smem) + len(hbm) + len(vmem)

    def body(*refs):
        kernel(*refs[:given], *refs[given + len(token) :])

    args = tuple(smem) + tuple(hbm) + tuple(vmem) + tuple(token)
    moved = sum(math.prod(a.shape) * a.dtype.itemsize for a in tuple(hbm) + tuple(vmem) + tuple(out_shape))
    return pl.pallas_call(
        body,
        out_shape=list(out_shape),
        in_specs=[SMEM] * len(smem) + [ANY] * len(hbm) + [VMEM] * len(vmem) + [ANY] * len(token),
        out_specs=[VMEM] * len(out_shape),
        scratch_shapes=list(scratch),
        compiler_params=pltpu.CompilerParams(vmem_limit_bytes=limit * MIB),
        cost_estimate=pl.CostEstimate(flops=flops, bytes_accessed=moved, transcendentals=0),
    )(*args)


def dot(a, b):
    return jnp.dot(a, b, preferred_element_type=F32)


def dot_nt(a, b):
    return lax.dot_general(a, b, (((1,), (1,)), ((), ())), preferred_element_type=F32)


def dot_tn(a, b):
    return lax.dot_general(a, b, (((0,), (0,)), ((), ())), preferred_element_type=F32)


def norm_mish(pre, gain):
    center = pre - jnp.mean(pre, axis=-1, keepdims=True)
    scale = lax.rsqrt(jnp.mean(center * center, axis=-1, keepdims=True) + 1e-05)
    normed = center * scale
    v = normed * gain
    e = jnp.exp(jnp.minimum(v, 20.0))
    n = e * (e + 2.0)
    r = 1.0 / (n + 2.0)
    t = n * r
    return v * t, normed, t + v * (4.0 * e * (1.0 + e)) * (r * r), scale


def norm_mish_back(upstream, normed, slope, scale, gain):
    dv = upstream * slope
    gain_grad = jnp.sum(dv * normed, axis=0, keepdims=True)
    a = dv * gain
    dpre = scale * (
        a
        - jnp.mean(a, axis=-1, keepdims=True)
        - normed * jnp.mean(a * normed, axis=-1, keepdims=True)
    )
    return dpre, gain_grad, jnp.sum(dpre, axis=0, keepdims=True)


def lanes(shape):
    return lax.broadcasted_iota(jnp.int32, shape, len(shape) - 1)


def column(block, at):
    return jnp.sum(jnp.where(lanes(block.shape) == at, block, 0.0), axis=-1, keepdims=True)


def spread_lanes(x, per, block, count, offset=0):
    lane = lanes(x.shape)
    out = jnp.zeros_like(x)
    for j in range(count):
        by = j * (block - per) + offset
        at = j * block + offset
        moved = pltpu.roll(x, by, 1) if by else x
        out = jnp.where((lane >= at) & (lane < at + per), moved, out)
    return out


def collect_lanes(x, per, block, count, offset=0):
    lane = lanes(x.shape)
    out = jnp.zeros_like(x)
    for j in range(count):
        by = j * (block - per) + offset
        moved = pltpu.roll(x, x.shape[1] - by, 1) if by else x
        out = jnp.where((lane >= j * per) & (lane < (j + 1) * per), moved, out)
    return out


def widen(x, width):
    return jnp.concatenate([x, jnp.zeros((x.shape[0], width - x.shape[1]), x.dtype)], axis=1)


def eights(block, join):
    lane = lanes(block.shape)
    for step in (1, 2, 4):
        partner = jnp.where(
            (lane & step) == 0, pltpu.roll(block, 128 - step, 1), pltpu.roll(block, step, 1)
        )
        block = join(block, partner)
    return block


def by_block(fn, *arrays):
    pieces = []
    for start in range(0, arrays[0].shape[1], 128):
        pieces.append(fn(*(a[:, start : start + 128] for a in arrays)))
    return jnp.concatenate(pieces, axis=1)


def simnorm_block(pre):
    e = jnp.exp(pre - eights(pre, jnp.maximum))
    return e / eights(e, jnp.add)


def simnorm_back_block(latent, upstream):
    return latent * (upstream - eights(latent * upstream, jnp.add))


VEC = {
    name: at
    for at, name in enumerate(
        ("eb1", "eg1", "eb2", "db1", "dg1", "db2", "dg2", "db3", "pb1", "pg1", "pb2", "pg2", "pb3")
    )
}


def load_packed(pieces, starts, packed, sems):
    copies = []
    for i, piece in enumerate(pieces):
        rows = piece.shape[0]
        to = packed.at[pl.ds(pl.multiple_of(starts[i], 32), rows), :]
        copies.append(pltpu.make_async_copy(piece, to, sems.at[i]))
    for c in copies:
        c.start()
    for c in copies:
        c.wait()


def pack_base_kernel(ublock, ids, d2, e2, d3, e1, d1, full, mine):
    rows, feat = d2.shape
    lat = e2.shape[1]
    a, b, c = feat, feat + lat, feat + 2 * lat
    full[:, :a] = d2[...]
    full[:, a:b] = e2[...]
    full[:, b:c] = d3[...]
    full[:ublock, c:] = jnp.zeros((ublock, feat), BF16)
    full[: d1.shape[0], c:] = d1[...]
    full[ublock:, c:] = e1[...]
    half = mine.shape[0]
    mine[...] = full[pl.ds(pl.multiple_of(ids[0] * half, 64), half), :]


def pack_policy_kernel(ids, p2, p3, p1, full, mine):
    rows, feat = p2.shape
    full[:, :feat] = p2[...]
    full[:, feat : feat + 128] = jnp.zeros((rows, 128), BF16)
    full[:, feat : feat + p3.shape[1]] = p3[...]
    full[:, feat + 128 :] = jnp.zeros((rows, feat), BF16)
    full[: p1.shape[0], feat + 128 :] = p1[...]
    half = mine.shape[0]
    mine[...] = full[pl.ds(pl.multiple_of(ids[0] * half, 64), half), :]


def pack_unit_kernel(ids, c2, c3, c1, r2, r3, r1, full, b2, b3, b1, sems):
    rows, feat = b2.shape

    @pl.when(ids[1] == 0)
    def _():
        for i, (src, dst) in enumerate(((c2, b2), (c3, b3), (c1, b1))):
            pltpu.make_async_copy(src.at[ids[0]], dst, sems.at[i]).start()

    @pl.when(ids[1] == 1)
    def _():
        for i, (src, dst) in enumerate(((r2, b2), (r3, b3), (r1, b1))):
            pltpu.make_async_copy(src, dst, sems.at[i]).start()

    for i, (src, dst) in enumerate(((r2, b2), (r3, b3), (r1, b1))):
        pltpu.make_async_copy(src, dst, sems.at[i]).wait()
    full[:, :feat] = b2[...]
    full[:, feat : feat + 128] = jnp.zeros((rows, 128), BF16)
    full[:, feat : feat + b3.shape[1]] = b3[...]
    full[:, feat + 128 :] = jnp.zeros((rows, feat), BF16)
    full[: b1.shape[0], feat + 128 :] = b1[...]


def forward_kernel(steps, narrow, joint, first, count, *refs):
    starts, pieces, refs = refs[0], refs[1 : 1 + count], refs[1 + count :]
    (
        obs, side, extra, target, vec,
        x256, x224, z0, z, rowloss, e_h, e_n, e_s, e_r, d_h1, d_n1, d_s1, d_r1, d_h2, d_n2, d_s2, d_r2,
        packed, sems,
    ) = refs
    rows = obs.shape[0]
    lat = z0.shape[1]
    feat = e_h.shape[1]
    block = feat // narrow
    ublock = x224.shape[1] // narrow
    load_packed(pieces, starts, packed, sems)
    d2 = packed.at[:, :feat]
    e2 = packed.at[:, feat : feat + lat]
    d3 = packed.at[:, feat + lat : feat + 2 * lat]
    w1 = packed.at[:, feat + 2 * lat :]

    def v(name, width=feat):
        return vec[VEC[name] : VEC[name] + 1, :width]

    def layer(x, w, bias, gain, h, n, s, r, at):
        out, normed, slope, scale = norm_mish(dot(x, w[...]) + v(bias), v(gain))
        low = out.astype(BF16)
        h[at, :] = low
        n[at, :] = normed
        s[at, :] = slope
        r[at, :] = scale
        return low

    first_in = spread_lanes(widen(obs[...].astype(F32), feat), first, block, narrow, ublock).astype(BF16)
    x256[steps * rows :, :] = first_in
    x1 = layer(first_in, w1, "eb1", "eg1", e_h, e_n, e_s, e_r, slice(0, rows))
    latent = by_block(simnorm_block, dot(x1, e2[...]) + v("eb2", lat))
    z0[...] = latent
    for t in range(steps):
        at = slice(t * rows, (t + 1) * rows)
        around = side[at, :].astype(F32)
        joined = jnp.concatenate([latent.astype(BF16).astype(F32), around], axis=1)
        wide_in = spread_lanes(widen(joined, feat), joint, block, narrow).astype(BF16)
        x256[at, :] = wide_in
        sent = spread_lanes(joined, joint, ublock, narrow)
        x224[at, :256] = (sent[:, :256] + extra[at, :].astype(F32)).astype(BF16)
        x224[at, 256:] = sent[:, 256:].astype(BF16)
        h1 = layer(wide_in, w1, "db1", "dg1", d_h1, d_n1, d_s1, d_r1, at)
        h2 = layer(h1, d2, "db2", "dg2", d_h2, d_n2, d_s2, d_r2, at)
        latent = by_block(simnorm_block, dot(h2, d3[...]) + v("db3", lat))
        z[at, :] = latent
        differ = latent - target[at, :]
        consistency = jnp.mean(differ * differ, axis=-1, keepdims=True)
        rowloss[at, :] = column(extra[at, :].astype(F32), joint + 2) * (20.0 * consistency)


def policy_kernel(narrow, joint, plain, act_at, count, *refs):
    starts, pieces, refs = refs[0], refs[1 : 1 + count], refs[1 + count :]
    (
        z0, z, emb, extra, noise, vec,
        xp, chosen_out, rowloss, p_h1, p_n1, p_s1, p_r1, p_h2, p_n2, p_s2, p_r2, pout,
        packed, sems,
    ) = refs
    feat = xp.shape[1]
    block = feat // narrow
    rows = z0.shape[0]
    load_packed(pieces, starts, packed, sems)

    def v(name, width=feat):
        return vec[VEC[name] : VEC[name] + 1, :width]

    def layer(x, w, bias, gain, h, n, s, r):
        out, normed, slope, scale = norm_mish(dot(x, w) + v(bias), v(gain))
        low = out.astype(BF16)
        h[...] = low
        n[...] = normed
        s[...] = slope
        r[...] = scale
        return low

    latent = jnp.concatenate([z0[...], z[: z.shape[0] - rows, :]], axis=0)
    latent = latent.astype(BF16).astype(F32)
    joined = widen(jnp.concatenate([latent, emb[...].astype(F32)], axis=1), feat)
    x = spread_lanes(joined, plain, block, narrow).astype(BF16)
    xp[...] = x
    h1 = layer(x, packed[:, feat + 128 :], "pb1", "pg1", p_h1, p_n1, p_s1, p_r1)
    h2 = layer(h1, packed[:, :feat], "pb2", "pg2", p_h2, p_n2, p_s2, p_r2)
    out = dot(h2, packed[:, feat : feat + 128]) + v("pb3", 128)
    pout[...] = out
    mu, raw = out, pltpu.roll(out, 120, 1)
    eps = noise[...]
    log_std = -10.0 + 6.0 * (jnp.tanh(raw) + 1.0)
    moved = mu + jnp.exp(log_std) * eps
    chosen = jnp.tanh(moved)
    bent = -2.0 * moved
    soft = jnp.maximum(bent, 0.0) + jnp.log1p(jnp.exp(-jnp.abs(bent)))
    density = -0.5 * eps * eps - log_std - 0.5 * math.log(2.0 * math.pi)
    terms = density - 2.0 * (math.log(2.0) - moved - soft)
    valid = lanes(terms.shape) < 8
    log_prob = jnp.sum(jnp.where(valid, terms, 0.0), axis=-1, keepdims=True)
    chosen_out[...] = pltpu.roll(jnp.where(valid, chosen, 0.0), act_at % 128, 1).astype(BF16)
    rowloss[...] = column(extra[...].astype(F32), joint + 2) * (0.1 * log_prob)


def unit_kernel(total_rows, bins, joint, act_at, plan, count, *refs):
    flags, to2, to1 = refs[:3]
    pieces = refs[3 : 3 + count]
    (
        x_in, chosen, vec,
        away, mine, x_out, h1_out, h2_out, dp1_out, dp2_out, dl_out, vgrad,
        w1, w2, w3, n1, s1, n2, s2, sems,
    ) = refs[3 + count :]
    step = pl.program_id(0)
    feat = w2.shape[0]
    width = x_in.shape[1]

    @pl.when(step == 0)
    def _():
        copies = []
        for i, (piece, at, rows, rows1) in enumerate(plan):
            ref = pieces[piece]
            src = pl.ds(at, rows)
            dst = pl.ds(pl.multiple_of(to2[i], 32), rows)
            copies.append((ref.at[src, :feat], w2.at[dst, :], 3 * i))
            copies.append((ref.at[src, feat : feat + 128], w3.at[dst, :], 3 * i + 1))
            dst = pl.ds(pl.multiple_of(to1[i], 16), rows1)
            copies.append((ref.at[pl.ds(at, rows1), feat + 128 :], w1.at[dst, :], 3 * i + 2))
        copies = [pltpu.make_async_copy(a, b, sems.at[i]) for a, b, i in copies]
        for c in copies:
            c.start()
        for c in copies:
            c.wait()
        vgrad[...] = jnp.zeros_like(vgrad)

    ce, probe, value = flags[0], flags[1], flags[2]
    b1, g1, b2, g2 = (vec[i : i + 1, :] for i in range(4))
    base = act_at // 128 * 128
    lane = lanes((x_in.shape[0], 128))
    acting = (lane >= act_at - base) & (lane < jnp.where(probe > 0.0, act_at - base + 8, 0))
    x = x_in[...]
    x_out[...] = x
    swapped = jnp.where(acting, chosen[...], x[:, base : base + 128])
    parts = [x[:, :base], swapped] + ([x[:, base + 128 :]] if base + 128 < width else [])
    h, normed, slope, scale1 = norm_mish(dot(jnp.concatenate(parts, axis=1), w1[...]) + b1, g1)
    n1[...] = normed
    s1[...] = slope
    h1 = h.astype(BF16)
    h1_out[...] = h1
    h, normed, slope, scale2 = norm_mish(dot(h1, w2[...]) + b2, g2)
    n2[...] = normed
    s2[...] = slope
    h2 = h.astype(BF16)
    h2_out[...] = h2
    logits = dot(h2, w3[...]) + vec[4:5, :128]
    valid = lane < bins
    side = x[:, :256].astype(F32)
    label = jnp.where(value > 0.5, column(side, joint + 1), column(side, joint))
    weight = column(side, joint + 2)
    hot = jnp.where(lane.astype(F32) == label, 1.0, 0.0)
    top = jnp.max(jnp.where(valid, logits, -jnp.inf), axis=-1, keepdims=True)
    e = jnp.where(valid, jnp.exp(logits - top), 0.0)
    total = jnp.sum(e, axis=-1, keepdims=True)
    p = e / total
    centers = -10.0 + 20.0 * lane.astype(F32) / (bins - 1)
    estimate = jnp.sum(p * centers, axis=-1, keepdims=True)
    entropy = top + jnp.log(total) - jnp.sum(hot * logits, axis=-1, keepdims=True)
    loss = weight * (ce * entropy - probe * estimate)
    dl = (weight / total_rows) * (ce * (p - hot) - probe * p * (centers - estimate))
    low = dl.astype(BF16)
    dl_out[...] = low
    vgrad[4:5, :128] += jnp.sum(dl, axis=0, keepdims=True)
    dp2, gg, bg = norm_mish_back(dot_nt(low, w3[...]), n2[...], s2[...], scale2, g2)
    vgrad[2:3, :] += bg
    vgrad[3:4, :] += gg
    low = dp2.astype(BF16)
    dp2_out[...] = low
    dp1, gg, bg = norm_mish_back(dot_nt(low, w2[...]), n1[...], s1[...], scale1, g1)
    vgrad[0:1, :] += bg
    vgrad[1:2, :] += gg
    low = dp1.astype(BF16)
    dp1_out[...] = low
    grad = dot_nt(low, w1[...])
    lane = lanes(grad.shape)
    drop = (lane >= jnp.where(probe > 0.0, 0, act_at)) & (lane < jnp.where(probe > 0.0, act_at, act_at + 8))
    high = loss.astype(BF16).astype(F32)
    grad = jnp.where(drop, 0.0, grad)
    grad = jnp.where(lane == joint, high, jnp.where(lane == joint + 1, loss - high, grad))
    grad = grad.astype(BF16)

    @pl.when(step < 4)
    def _():
        away[...] = grad

    @pl.when(step >= 4)
    def _():
        mine[...] = grad


def add_kernel(*refs):
    total = refs[0][...].astype(F32)
    for ref in refs[1:-1]:
        total = total + ref[...].astype(F32)
    refs[-1][...] = total.astype(refs[-1].dtype)


def split_sum_kernel(a, b, *outs):
    rows = a.shape[0] // len(outs)
    for i, out in enumerate(outs):
        at = slice(i * rows, (i + 1) * rows)
        out[...] = (a[at, :].astype(F32) + b[at, :].astype(F32)).astype(out.dtype)


def policy_back_kernel(
    total_rows, narrow, joint, plain, act_at, count, *refs,
):
    starts, pieces, refs = refs[0], refs[1 : 1 + count], refs[1 + count :]
    (
        da, db, dc, extra, noise, pout, vec, n1, s1, r1, n2, s2, r2,
        dxs, dp1_out, dp2_out, do_out, demb, rowloss, vgrad,
        packed, sems,
    ) = refs
    feat = n1.shape[1]
    block = feat // narrow
    load_packed(pieces, starts, packed, sems)

    def v(name, width=feat):
        return vec[VEC[name] : VEC[name] + 1, :width]

    total = da[...].astype(F32) + db[...].astype(F32) + dc[...].astype(F32)
    dxs[...] = total
    rowloss[...] = column(total[:, :256], joint) + column(total[:, :256], joint + 1)
    out = pout[...]
    raw = pltpu.roll(out, 120, 1)
    eps = noise[...]
    valid = lanes(raw.shape) < 8
    bent = jnp.tanh(raw)
    spread = jnp.exp(-10.0 + 6.0 * (bent + 1.0))
    chosen = jnp.tanh(out + spread * eps)
    base = act_at // 128 * 128
    dchosen = pltpu.roll(total[:, base : base + 128], (128 - act_at % 128) % 128, 1)
    g = column(extra[...].astype(F32), joint + 2) * (0.1 / total_rows)
    dmoved = jnp.where(valid, dchosen * (1.0 - chosen * chosen) + 2.0 * g * chosen, 0.0)
    draw = jnp.where(valid, (dmoved * spread * eps - g) * 6.0 * (1.0 - bent * bent), 0.0)
    do = dmoved + pltpu.roll(draw, 8, 1)
    low = do.astype(BF16)
    do_out[...] = low
    vgrad[...] = jnp.zeros_like(vgrad)
    vgrad[4:5, :128] = jnp.sum(do, axis=0, keepdims=True)
    up = dot_nt(low, packed[:, feat : feat + 128])
    dp2, gg, bg = norm_mish_back(up, n2[...], s2[...], r2[...], v("pg2"))
    vgrad[2:3, :] = bg
    vgrad[3:4, :] = gg
    low = dp2.astype(BF16)
    dp2_out[...] = low
    dp1, gg, bg = norm_mish_back(dot_nt(low, packed[:, :feat]), n1[...], s1[...], r1[...], v("pg1"))
    vgrad[0:1, :] = bg
    vgrad[1:2, :] = gg
    low = dp1.astype(BF16)
    dp1_out[...] = low
    down = collect_lanes(dot_nt(low, packed[:, feat + 128 :]), plain, block, narrow)
    lat = feat - 256
    demb[...] = down[:, lat : lat + 128]


def chain_back_kernel(steps, narrow, joint, first, total_rows, count, *refs):
    starts, pieces, refs = refs[0], refs[1 : 1 + count], refs[1 + count :]
    (
        dxs, extra, target, z0, z, vec, e_n, e_s, e_r, d_n1, d_s1, d_r1, d_n2, d_s2, d_r2,
        p1_out, p2_out, p3_out, e2_out, demb, obs_grad, vgrad,
        packed, sems,
    ) = refs
    rows, lat = z0.shape
    feat = d_n1.shape[1]
    block = feat // narrow
    ublock = dxs.shape[1] // narrow
    load_packed(pieces, starts, packed, sems)
    d2 = packed.at[:, :feat]
    e2 = packed.at[:, feat : feat + lat]
    d3 = packed.at[:, feat + lat : feat + 2 * lat]
    w1 = packed.at[:, feat + 2 * lat :]

    def v(name, width=feat):
        return vec[VEC[name] : VEC[name] + 1, :width]

    vgrad[...] = jnp.zeros_like(vgrad)
    carried = jnp.zeros((rows, lat), F32)
    for t in range(steps - 1, -1, -1):
        at = slice(t * rows, (t + 1) * rows)
        here = z[at, :]
        weight = column(extra[at, :].astype(F32), joint + 2)
        up = carried + (weight * (40.0 / lat / total_rows)) * (here - target[at, :])
        dp3 = by_block(simnorm_back_block, here, up)
        vgrad[7:8, :lat] += jnp.sum(dp3, axis=0, keepdims=True)
        low = dp3.astype(BF16)
        p3_out[at, :] = low
        dp2, gg, bg = norm_mish_back(
            dot_nt(low, d3[...]), d_n2[at, :], d_s2[at, :], d_r2[at, :], v("dg2")
        )
        vgrad[5:6, :] += bg
        vgrad[6:7, :] += gg
        low = dp2.astype(BF16)
        p2_out[at, :] = low
        dp1, gg, bg = norm_mish_back(
            dot_nt(low, d2[...]), d_n1[at, :], d_s1[at, :], d_r1[at, :], v("dg1")
        )
        vgrad[3:4, :] += bg
        vgrad[4:5, :] += gg
        low = dp1.astype(BF16)
        p1_out[at, :] = low
        joined = collect_lanes(dot_nt(low, w1[...]), joint, block, narrow)[:, : lat + 128]
        joined = joined + collect_lanes(dxs[at, :], joint, ublock, narrow)
        carried = joined[:, :lat]
        demb[at, :] = joined[:, lat:]
    dp2 = by_block(simnorm_back_block, z0[...], carried)
    vgrad[2:3, :lat] = jnp.sum(dp2, axis=0, keepdims=True)
    low = dp2.astype(BF16)
    e2_out[...] = low
    dp1, gg, bg = norm_mish_back(dot_nt(low, e2[...]), e_n[...], e_s[...], e_r[...], v("eg1"))
    vgrad[0:1, :] = bg
    vgrad[1:2, :] = gg
    low = dp1.astype(BF16)
    p1_out[steps * rows :, :] = low
    down = collect_lanes(dot_nt(low, w1[...]), first, block, narrow, ublock)
    obs_grad[...] = down[:, : obs_grad.shape[1]] * total_rows


HALVES = ((3, 0), (1, 0), (3, 1), (2, 1), (1, 1), (2, 0), (0, 0), (0, 1))


def base_grad_kernel(steps, with_vectors, starts, h1, p2, eh, ep2, h2, p3, x, p1, cemb, pemb, hot, cvec, *outs):
    *outs, vb = outs
    feat = h1.shape[1]
    lat = p3.shape[1]
    if with_vectors:
        embed = cemb[...]
        embed = pltpu.roll(embed, 120, 1) + pemb[...]
        rows = hot.shape[0]
        embed = sum(embed[t * rows : (t + 1) * rows, :] for t in range(steps))
        embed = jnp.where(lanes(embed.shape) < 96, embed, 0.0)
        table = lax.dot_general(
            hot[...], embed, (((0,), (0,)), ((), ())), preferred_element_type=F32,
            precision=lax.Precision.HIGHEST,
        )
        vb[...] = jnp.zeros_like(vb)
        for i in range(8):
            vb[8 * i : 8 * i + 8, :] = cvec[:, 128 * i : 128 * (i + 1)]
        vb[64:192, :] = table
    size = 128
    for c in range(starts.shape[0]):
        at = pl.ds(pl.multiple_of(starts[c], size), size)
        parts = [
            dot_tn(h1[:, at], p2[...]),
            dot_tn(eh[:, at], ep2[...]),
            dot_tn(h2[:, at], p3[...]),
            dot_tn(x[:, at], p1[...]),
        ]
        if with_vectors:
            parts.append(vb[pl.ds(pl.multiple_of(lax.rem(starts[c], 2 * size), size), size), :])
        store_chunk(outs, c, size, jnp.concatenate(parts, axis=1).astype(BF16))


def store_chunk(outs, c, size, value):
    if len(outs) == 1:
        outs[0][c] = value
        return
    out, k = outs[c // 4], c % 4
    half = size // 2
    for i, (dest, part) in enumerate(HALVES):
        if dest == k:
            out[i] = value[part * half : (part + 1) * half, :]


def policy_grad_kernel(ublock, with_vectors, starts, h1, p2, h2, do, x, p1, pvec, *outs):
    feat = h1.shape[1]
    size = 128
    for c in range(starts.shape[0]):
        at = pl.ds(pl.multiple_of(starts[c], size), size)
        rest = dot_tn(x[:, at], p1[...])
        if with_vectors:
            above = ublock - size
            around = [jnp.zeros((above, feat), F32), pvec[...], jnp.zeros((size - above - 8, feat), F32)]
            second = lax.rem(starts[c], 2 * size) // size
            rest = rest + jnp.concatenate(around, axis=0) * second.astype(F32)
        parts = [dot_tn(h1[:, at], p2[...]), dot_tn(h2[:, at], do[...]), rest]
        store_chunk(outs, c, size, jnp.concatenate(parts, axis=1).astype(BF16))


def unit_grad_kernel(narrow, with_vectors, starts, x, h1, h2, dp1, dp2, dl, uvec, *outs):
    *outs, w1 = outs
    feat = h1.shape[1]
    block = feat // narrow
    ublock = x.shape[1] // narrow
    w1[...] = dot_tn(x[...], dp1[...])
    for c in range(narrow):
        at = pl.ds(pl.multiple_of(starts[c] * block, 128), block)
        rows = pl.ds(pl.multiple_of(starts[c] * ublock, 16), ublock)
        below = [w1[rows, :]]
        if with_vectors:
            below += [uvec[...], jnp.zeros((block - ublock - 8, feat), F32)]
        else:
            below += [jnp.zeros((block - ublock, feat), F32)]
        parts = [dot_tn(h1[:, at], dp2[...]), dot_tn(h2[:, at], dl[...]), jnp.concatenate(below, axis=0)]
        value = jnp.concatenate(parts, axis=1).astype(BF16)
        if len(outs) == 1:
            outs[0][c] = value
            continue
        half = block // 2
        for i, (dest, part) in enumerate(HALVES):
            if dest == c:
                piece = value[part * half : (part + 1) * half, :]
                if i in (4, 5):
                    outs[i - 2][...] = piece
                else:
                    outs[i // 2 if i < 4 else 4][i % 2] = piece


def core_sum_kernel(mine, other, x1, y1, m1, m2, m0):
    for i, out in enumerate((x1.at[0], x1.at[1], y1.at[0], y1.at[1], m1, m2, m0.at[0], m0.at[1])):
        out[...] = (mine[i].astype(F32) + other[i].astype(F32)).astype(BF16)


def narrow_mid_kernel(m1, m2, rx, ry, sx, sy):
    sx[...] = (m1[...].astype(F32) + ry[0].astype(F32)).astype(BF16)
    sy[...] = (m2[...].astype(F32) + rx[0].astype(F32)).astype(BF16)


def narrow_end_kernel(m0, rx, ry, rx2, ry2, a, b):
    a[...] = (m0[0].astype(F32) + rx[1].astype(F32) + ry2[...].astype(F32)).astype(BF16)
    b[...] = (m0[1].astype(F32) + ry[1].astype(F32) + rx2[...].astype(F32)).astype(BF16)


def narrow_cut_kernel(ids, m0, rx, ry, rx2, ry2, b11, b10, b01, b00, t):
    half = m0.shape[1]
    t[:half, :] = m0[0].astype(F32) + rx[1].astype(F32) + ry2[...].astype(F32)
    t[half:, :] = m0[1].astype(F32) + ry[1].astype(F32) + rx2[...].astype(F32)
    low, high = ids[1], ids[2]
    size = half // 2
    for out, dl, dh in ((b11, 1, 1), (b10, 1, 0), (b01, 0, 1), (b00, 0, 0)):
        l = low + dl - 2 * low * dl
        h = high + dh - 2 * high * dh
        out[...] = t[pl.ds(pl.multiple_of(h * half + l * size, 32), size), :].astype(BF16)


def base_end_kernel(lat, joint, first, ublock, ids, *refs):
    pieces, (d2, e2, d3, d1, e1, vb, w1) = refs[:8], refs[8:]
    size = pieces[0].shape[0]
    feat = d2.shape[1]
    a, b, c = feat, feat + lat, feat + 2 * lat
    for i, piece in enumerate(pieces):
        rows = pl.ds(pl.multiple_of(ids[4 + i], 32), size)
        d2[rows, :] = piece[:, :a].astype(F32)
        e2[rows, :] = piece[:, a:b].astype(F32)
        d3[rows, :] = piece[:, b:c].astype(F32)
        w1[rows, :] = piece[:, c : c + feat].astype(F32)
        vb[rows, :] = piece[:, c + feat :].astype(F32)
    d1[...] = w1[:joint, :]
    e1[...] = w1[ublock : ublock + first, :]


def policy_end_kernel(plain, ublock, ids, *refs):
    pieces, (p2, p3, p1, vec, w1, w3) = refs[:8], refs[8:]
    size = pieces[0].shape[0]
    feat = p2.shape[1]
    for i, piece in enumerate(pieces):
        rows = pl.ds(pl.multiple_of(ids[4 + i], 32), size)
        p2[rows, :] = piece[:, :feat].astype(F32)
        w3[rows, :] = piece[:, feat : feat + 128].astype(F32)
        w1[rows, :] = piece[:, feat + 128 :].astype(F32)
    p3[...] = w3[:, : p3.shape[1]]
    p1[...] = w1[:plain, :]
    vec[...] = w1[ublock : ublock + 8, :]


def unit_end_kernel(joint, ublock, bins, ids, *refs):
    given, (c2, c3, c1, r2, r3, r1, vec, buf, sems) = refs[:28], refs[28:]
    feat = c2.shape[2]
    half = buf.shape[2] // 2
    z = 2 * ids[2] + ids[1]
    table = ((0, 1, 2, 3), (5, 4, 0, 1), (6, 5, 4, 0))
    waits = []
    for s, row in enumerate(table):
        for side in (0, 1):
            core = ids[0] + side - 2 * ids[0] * side
            for part in (0, 1):
                to = buf.at[s, core, pl.ds(part * half, half), :]
                sem = sems.at[(s * 2 + side) * 2 + part]
                for k, at in enumerate(row):

                    @pl.when(z == k)
                    def _(at=at, to=to, sem=sem, side=side, part=part):
                        pltpu.make_async_copy(given[(side * 7 + at) * 2 + part], to, sem).start()

                waits.append(pltpu.make_async_copy(given[part], to, sem))
    for w in waits:
        w.wait()
    for i in range(6):
        block = buf.at[i // 2, i % 2]
        out2, out3, out1 = (r2, r3, r1) if i == 5 else (c2.at[i], c3.at[i], c1.at[i])
        out2[...] = block[:, :feat].astype(F32)
        out3[...] = block[:, feat : feat + bins].astype(F32)
        out1[...] = block[:joint, feat + 128 :].astype(F32)
        vec[i] = block[ublock : ublock + 16, feat + 128 :].astype(F32)


def swap(array, axis, size, bit):
    return lax.ppermute(array, axis, [(i, i ^ bit) for i in range(size)])


def shift(array, axis, size, by, sources):
    return lax.ppermute(array, axis, [(i, i + by) for i in range(size) if i // 2 in sources])


def slot_groups(wide):
    return [list(range(i, i + SLOTS)) for i in range(0, wide, SLOTS)]


def reduce_core(mine, away, wide):
    other = swap(away, "wide", wide, 1)
    half, width = mine.shape[1:]
    one, two = shape((half, width), BF16), shape((2, half, width), BF16)
    return call(core_sum_kernel, [two, two, one, one, two], vmem=(mine, other))


def reduce_narrow(pieces, narrow, ids=None):
    x1, y1, m1, m2, m0 = pieces
    rx, ry = swap(x1, "narrow", narrow, 1), swap(y1, "narrow", narrow, 2)
    one = shape(m1.shape, BF16)
    sx, sy = call(narrow_mid_kernel, [one, one], vmem=(m1, m2, rx, ry))
    rx2, ry2 = swap(sx, "narrow", narrow, 1), swap(sy, "narrow", narrow, 2)
    if ids is None:
        return call(narrow_end_kernel, [one, one], vmem=(m0, rx, ry, rx2, ry2))
    half, width = m1.shape
    return call(
        narrow_cut_kernel, [shape((half // 2, width), BF16)] * 4, smem=(ids,), vmem=(m0, rx, ry, rx2, ry2),
        scratch=[pltpu.VMEM((2 * half, width), F32)],
    )


def reduce_line(pieces, wide):
    b11, b10, b01, b00 = pieces
    one = [shape(b00.shape, BF16)]
    r11 = swap(b11, "wide", wide, 2)
    (c01,) = call(add_kernel, one, vmem=(b01, r11))
    r01 = swap(c01, "wide", wide, 4)
    r10 = swap(b10, "wide", wide, 2)
    (f,) = call(add_kernel, one, vmem=(b00, r01, r10))
    f4 = swap(f, "wide", wide, 4)
    f2 = swap(f, "wide", wide, 2)
    f42 = swap(f4, "wide", wide, 2)
    mine = [f, f2, f4, f42]
    return mine + [swap(a, "wide", wide, 1) for a in mine]


def gather_halves(a, b, wide):
    out = []
    for part in (a, b):
        r1 = shift(part, "wide", wide, 2, (0, 2))
        l1 = shift(part, "wide", wide, -2, (2, 3))
        r2 = shift(r1, "wide", wide, 2, (1,))
        l2 = shift(l1, "wide", wide, -2, (1, 2))
        r3 = shift(r2, "wide", wide, 2, (2,))
        l3 = shift(l2, "wide", wide, -2, (1,))
        out.append((part, r1, r2, r3, l1, l2, l3))
    mine = [piece for pair in zip(*out) for piece in pair]
    return mine + [swap(piece, "wide", wide, 1) for piece in mine]


def pad_to(array, rows, columns):
    return jnp.pad(array, ((0, rows - array.shape[0]), (0, columns - array.shape[1])))


def gather_shared(full, mine, me, core, narrow, wide):
    block = full.shape[0]
    if narrow != 4:
        return [lax.all_gather(full, "narrow", axis=0, tiled=True)], jnp.zeros((1,), jnp.int32)
    half = block // 2
    quarter = half // 2
    p1, p2 = swap(mine, "narrow", narrow, 1), swap(mine, "narrow", narrow, 2)
    p3a = swap(p1[:quarter], "narrow", narrow, 2)
    p3b = swap(p2[quarter:], "narrow", narrow, 1)
    got = [p1, p2, p3a, p3b]
    starts = [me * block]
    for c in (core, 1 - core):
        at = [(me ^ k) * block + c * half for k in (1, 2, 3)]
        starts += at + [at[2] + quarter]
    return [full] + got + [swap(a, "wide", wide, 1) for a in got], jnp.stack(starts)


def on_device(
    wide, narrow, obs, actions, target_latents, noise, horizon, step_mask, task_ids, reward_bins, value_bins,
    task_table, encoder_first, encoder_second, dynamics_first, dynamics_second, dynamics_third,
    reward_first, reward_second, reward_third, critic_first, critic_second, critic_third,
    policy_first, policy_second, policy_third, encoder_bias, encoder_gain, dynamics_bias, dynamics_gain,
    reward_bias, reward_gain, critic_bias, critic_gain, policy_bias, policy_gain,
):
    fast = wide == SLOTS and narrow == 4
    rows, steps, act = actions.shape
    tall = rows * steps
    total_rows = rows * wide * narrow
    lat = encoder_second.shape[1]
    feat = encoder_first.shape[1]
    tasks, emb = task_table.shape
    bins = reward_third.shape[-1]
    heads = critic_first.shape[0]
    first = encoder_first.shape[0]
    joint = dynamics_first.shape[0]
    plain = policy_first.shape[0]
    block = encoder_second.shape[0]
    width = lat + 128
    ublock = width // narrow
    act_at = lat // joint * ublock + lat % joint
    wide_at = lax.axis_index("wide")
    me = lax.axis_index("narrow")
    core = wide_at % 2
    low, high = wide_at // 2 % 2, wide_at // 4 % 2
    slot = wide_at % SLOTS
    head = jnp.asarray(SLOT_HEAD, jnp.int32)[slot]
    is_probe = jnp.asarray(SLOT_PROBE, jnp.int32)[slot]
    is_reward = jnp.asarray(SLOT_REWARD, jnp.int32)[slot]
    at_z = [(core, high, low), (core, high, 1 - low), (core, 1 - high, low), (core, 1 - high, 1 - low)]
    at_z += [(1 - c, h, l) for c, h, l in at_z]
    ids = jnp.stack(
        [core, low, high, me] + [c * (block // 2) + h * (block // 4) + l * (block // 8) for c, h, l in at_z]
    ).astype(jnp.int32)

    base_width = 2 * feat + 2 * lat
    net_width = 2 * feat + 128
    full, mine = call(
        functools.partial(pack_base_kernel, ublock),
        [shape((block, base_width), BF16), shape((block // 2, base_width), BF16)],
        smem=(ids,),
        vmem=(dynamics_second, encoder_second, dynamics_third, encoder_first, dynamics_first),
    )
    base, base_at = gather_shared(full, mine, me, core, narrow, wide)
    full, mine = call(
        pack_policy_kernel,
        [shape((block, net_width), BF16), shape((block // 2, net_width), BF16)],
        smem=(ids,),
        vmem=(policy_second, policy_third, policy_first),
        token=base[3:5],
    )
    acting, acting_at = gather_shared(full, mine, me, core, narrow, wide)
    (unit,) = call(
        pack_unit_kernel,
        [shape((block, net_width), BF16)],
        smem=(jnp.stack([head, is_reward]),),
        hbm=(critic_second, critic_third, critic_first, reward_second, reward_third, reward_first),
        token=acting[1:3],
        scratch=[
            pltpu.VMEM((block, feat), BF16),
            pltpu.VMEM((block, bins), BF16),
            pltpu.VMEM((joint, feat), BF16),
            pltpu.SemaphoreType.DMA((3,)),
        ],
    )
    if narrow == 4:
        half = block // 2
        u1, u2 = swap(unit, "narrow", narrow, 1), swap(unit, "narrow", narrow, 2)
        u3a, u3b = swap(u1[:half], "narrow", narrow, 2), swap(u2[half:], "narrow", narrow, 1)
        units = [unit, u1, u2, u3a, u3b]
        plan = [(0, 0, block, ublock), (1, 0, block, ublock), (2, 0, block, ublock)]
        plan += [(3, 0, half, half), (4, 0, half, ublock - half)]
        to2 = jnp.stack([me * block, (me ^ 1) * block, (me ^ 2) * block, (me ^ 3) * block, (me ^ 3) * block + half])
        to1 = jnp.stack([me * ublock, (me ^ 1) * ublock, (me ^ 2) * ublock, (me ^ 3) * ublock, (me ^ 3) * ublock + half])
    else:
        units = [lax.all_gather(unit, "narrow", axis=0, tiled=True)]
        plan = [(0, j * block, block, ublock) for j in range(narrow)]
        to2 = jnp.arange(narrow, dtype=jnp.int32) * block
        to1 = jnp.arange(narrow, dtype=jnp.int32) * ublock

    def line(vector, start, size):
        return jnp.pad(vector[start : start + size], (0, feat - size))

    vec = jnp.stack(
        [
            line(encoder_bias, 0, feat),
            encoder_gain,
            line(encoder_bias, feat, lat),
            line(dynamics_bias, 0, feat),
            line(dynamics_gain, 0, feat),
            line(dynamics_bias, feat, feat),
            line(dynamics_gain, feat, feat),
            line(dynamics_bias, 2 * feat, lat),
            line(policy_bias, 0, feat),
            line(policy_gain, 0, feat),
            line(policy_bias, feat, feat),
            line(policy_gain, feat, feat),
            line(policy_bias, 2 * feat, 2 * act),
        ]
        + [jnp.zeros((feat,), F32)] * 3
    )

    def pick(values, reward):
        return jnp.where(is_reward == 1, reward, lax.dynamic_index_in_dim(values, head, 0, keepdims=False))

    unit_bias = pick(critic_bias, reward_bias)
    unit_gain = pick(critic_gain, reward_gain)
    unit_vec = jnp.stack(
        [
            line(unit_bias, 0, feat),
            line(unit_gain, 0, feat),
            line(unit_bias, feat, feat),
            line(unit_gain, feat, feat),
            line(unit_bias, 2 * feat, bins),
        ]
        + [jnp.zeros((feat,), F32)] * 3
    )

    def by_step(array):
        return jnp.swapaxes(array, 0, 1).reshape((tall,) + array.shape[2:])

    onehot = (task_ids[:, None] == jnp.arange(128, dtype=jnp.int32)[None, :]).astype(F32)
    embed = jnp.dot(onehot[:, :tasks], task_table, precision=lax.Precision.HIGHEST).astype(BF16)
    moment = jnp.arange(steps, dtype=jnp.int32)[None, :]
    weighting = (
        jnp.where(moment < horizon[:, None], 1.0, 0.0)
        * step_mask.astype(F32)
        * (0.5 ** moment.astype(F32))
    )
    embeds = jnp.tile(embed, (steps, 1))
    side = jnp.concatenate(
        [by_step(actions).astype(BF16), embeds, jnp.zeros((tall, 128 - act - emb), BF16)], axis=1
    )
    emb_in = pad_to(embeds, tall, 128)
    lane = jnp.arange(256, dtype=jnp.int32)[None, :]
    extra = jnp.where(
        lane == joint,
        by_step(reward_bins)[:, None].astype(BF16),
        jnp.where(
            lane == joint + 1,
            by_step(value_bins)[:, None].astype(BF16),
            jnp.where(lane == joint + 2, by_step(weighting)[:, None].astype(BF16), 0),
        ),
    )
    eps = pad_to(by_step(noise), tall, 128)
    target = by_step(target_latents)

    wide_f = shape((tall, feat), F32)
    wide_b = shape((tall, feat), BF16)
    one = shape((tall, 1), F32)
    kept = [wide_b, wide_f, wide_f, one]
    room = [pltpu.VMEM((narrow * block, base_width), BF16), pltpu.SemaphoreType.DMA((len(base),))]
    (
        x256, x224, z0, z, rowloss, e_h, e_n, e_s, e_r, d_h1, d_n1, d_s1, d_r1, d_h2, d_n2, d_s2, d_r2,
    ) = call(
        functools.partial(forward_kernel, steps, narrow, joint, first, len(base)),
        [
            shape((tall + rows, feat), BF16), shape((tall, width), BF16), shape((rows, lat), F32), shape((tall, lat), F32), one,
            shape((rows, feat), BF16), shape((rows, feat), F32), shape((rows, feat), F32), shape((rows, 1), F32),
        ] + kept * 2,
        smem=(base_at,), hbm=base, vmem=(obs, side, extra, target, vec), scratch=room,
        flops=2 * tall * 3 * feat * feat,
    )
    net_room = [pltpu.VMEM((narrow * block, net_width), BF16), pltpu.SemaphoreType.DMA((len(acting),))]
    (
        xp, chosen, p_rowloss, p_h1, p_n1, p_s1, p_r1, p_h2, p_n2, p_s2, p_r2, pout,
    ) = call(
        functools.partial(policy_kernel, narrow, joint, plain, act_at, len(acting)),
        [wide_b, shape((tall, 128), BF16), one] + kept * 2 + [shape((tall, 128), F32)],
        smem=(acting_at,), hbm=acting, vmem=(z0, z, emb_in, extra, eps, vec), scratch=net_room,
        flops=2 * tall * 2 * feat * feat,
    )

    def gather_rows(array):
        if not fast:
            return lax.all_gather(
                array, "wide", axis=0, axis_index_groups=slot_groups(wide), tiled=True
            )
        by4, by2 = swap(array, "wide", wide, 4), swap(array, "wide", wide, 2)
        by6 = swap(by4, "wide", wide, 2)
        mine = [array, by4, by2, by6]
        return jnp.concatenate([swap(a, "wide", wide, 1) for a in mine] + mine, axis=0)

    x = gather_rows(x224)
    group_chosen = gather_rows(chosen)
    ce = jnp.where(is_reward == 1, 0.1, jnp.where(is_probe == 1, 0.0, 0.1 / heads))
    flags = jnp.stack([ce, jnp.where(is_probe == 1, 0.5, 0.0), jnp.where(is_reward == 1, 0.0, 1.0)])
    away, mine, x, h1, h2, dp1, dp2, dl, unit_vgrad = run_unit(
        functools.partial(unit_kernel, total_rows, bins, joint, act_at, plan, len(units)),
        (flags.astype(F32), to2, to1), units, x, group_chosen, unit_vec, tall, feat, len(plan),
    )
    if fast:
        other = swap(away, "wide", wide, 1)
        part = shape((tall, width), BF16)
        b00, b01, b10, b11 = call(split_sum_kernel, [part] * 4, vmem=(mine, other))
        r11 = swap(b11, "wide", wide, 2)
        (c01,) = call(add_kernel, [part], vmem=(b01, r11))
        sums = (b00, swap(c01, "wide", wide, 4), swap(b10, "wide", wide, 2))
    else:
        both = jnp.concatenate([away, mine], axis=0).reshape(SLOTS, tall, width)
        pieces = lax.all_to_all(both, "wide", 0, 0, axis_index_groups=slot_groups(wide))
        nothing = jnp.zeros((tall, width), BF16)
        sums = (jnp.sum(pieces.astype(F32), axis=0), nothing, nothing)

    dxs, pp1, pp2, po, pemb, u_rowloss, p_vgrad = call(
        functools.partial(policy_back_kernel, total_rows, narrow, joint, plain, act_at, len(acting)),
        [
            shape((tall, width), F32), wide_b, wide_b, shape((tall, 128), BF16), shape((tall, 128), F32), one,
            shape((8, feat), F32),
        ],
        smem=(acting_at,), hbm=acting,
        vmem=sums + (extra, eps, pout, vec, p_n1, p_s1, p_r1, p_n2, p_s2, p_r2), scratch=net_room,
        flops=2 * tall * 2 * feat * feat,
    )
    row_loss = jnp.sum((rowloss + p_rowloss + u_rowloss)[:, 0].reshape(steps, rows), axis=0)
    cp1, cp2, cp3, ep2, cemb, obs_grad, c_vgrad = call(
        functools.partial(chain_back_kernel, steps, narrow, joint, first, total_rows, len(base)),
        [
            shape((tall + rows, feat), BF16), wide_b, shape((tall, lat), BF16), shape((rows, lat), BF16),
            shape((tall, 128), F32), shape(obs.shape, F32), shape((8, feat), F32),
        ],
        smem=(base_at,), hbm=base,
        vmem=(dxs, extra, target, z0, z, vec, e_n, e_s, e_r, d_n1, d_s1, d_r1, d_n2, d_s2, d_r2), scratch=room,
        flops=2 * tall * 3 * feat * feat,
    )

    halves = block // 2
    if fast:
        order = jnp.stack([me, me ^ 1, me ^ 2, me ^ 3])
        chunks = jnp.concatenate([order * block + core * halves, order * block + (1 - core) * halves])
        two, single = shape((2, halves, net_width), BF16), shape((halves, net_width), BF16)
        unit_shape = [two, two, single, single, two]
        base_shape = [shape((8, halves // 2, base_width + 128), BF16)] * 2
        policy_shape = [shape((8, halves // 2, net_width), BF16)] * 2
    else:
        order = jnp.arange(narrow, dtype=jnp.int32)
        chunks = jnp.arange(narrow * block // 128, dtype=jnp.int32) * 128
        unit_shape = [shape((narrow, block, net_width), BF16)]
        base_shape = [shape((narrow * block // 128, 128, base_width), BF16)]
        policy_shape = [shape((narrow * block // 128, 128, net_width), BF16)]
    g_unit = call(
        functools.partial(unit_grad_kernel, narrow, fast), unit_shape,
        smem=(order,), vmem=(x, h1, h2, dp1, dp2, dl, unit_vgrad),
        scratch=[pltpu.VMEM((width, feat), F32)], flops=4 * SLOTS * tall * feat * feat,
    )
    g_policy = call(
        functools.partial(policy_grad_kernel, ublock, fast), policy_shape,
        smem=(chunks,), vmem=(p_h1, pp2, p_h2, po, xp, pp1, p_vgrad), flops=4 * tall * feat * feat,
    )
    g_base = call(
        functools.partial(base_grad_kernel, steps, fast), base_shape,
        smem=(chunks,), vmem=(d_h1, cp2, e_h, ep2, d_h2, cp3, x256, cp1, cemb, pemb, onehot, c_vgrad),
        scratch=[pltpu.VMEM((256, 128), F32)], flops=6 * tall * feat * feat,
    )

    def biases(s):
        return jnp.concatenate([s[0], s[2], s[4, :bins]])

    def gains(s):
        return jnp.concatenate([s[1], s[3]])

    if fast:
        a, b = reduce_narrow(g_unit, narrow)
        graded = gather_halves(a, b, wide)
        policy_parts = reduce_line(reduce_narrow(reduce_core(*g_policy, wide), narrow, ids), wide)
        base_parts = reduce_line(reduce_narrow(reduce_core(*g_base, wide), narrow, ids), wide)
        c2, c3, c1, r2, r3, r1, unit_rows = call(
            functools.partial(unit_end_kernel, joint, ublock, bins),
            [
                shape((heads, block, feat), F32), shape((heads, block, bins), F32), shape((heads, joint, feat), F32),
                shape((block, feat), F32), shape((block, bins), F32), shape((joint, feat), F32), shape((6, 16, feat), F32),
            ],
            smem=(ids,), hbm=graded,
            scratch=[pltpu.VMEM((3, 2, block, net_width), BF16), pltpu.SemaphoreType.DMA((12,))],
        )
        p2, p3, p1, s_pol = call(
            functools.partial(policy_end_kernel, plain, ublock),
            [shape((block, feat), F32), shape((block, 2 * act), F32), shape((plain, feat), F32), shape((8, feat), F32)],
            smem=(ids,), vmem=policy_parts,
            scratch=[pltpu.VMEM((block, feat), F32), pltpu.VMEM((block, 128), F32)],
        )
        d2, e2, d3, d1, e1, vb = call(
            functools.partial(base_end_kernel, lat, joint, first, ublock),
            [
                shape((block, feat), F32), shape((block, lat), F32), shape((block, lat), F32), shape((joint, feat), F32),
                shape((first, feat), F32), shape((block, 128), F32),
            ],
            smem=(ids,), vmem=base_parts, scratch=[pltpu.VMEM((block, feat), F32)],
        )
        s_chain = jnp.swapaxes(vb[:64].reshape(8, 8, 128), 0, 1).reshape(8, feat)
        grad_table = vb[64 : 64 + tasks, :emb]
        critic_bias_grad = jnp.stack([biases(unit_rows[i]) for i in range(heads)])
        critic_gain_grad = jnp.stack([gains(unit_rows[i]) for i in range(heads)])
        reward_rows = unit_rows[5]
    else:
        def scatter(array):
            array = array.reshape((narrow, block, array.shape[-1]))
            return lax.psum_scatter(array, "narrow", scatter_dimension=0, tiled=False)

        g_unit = scatter(g_unit[0])
        if wide != SLOTS:
            same = [list(range(i, wide, SLOTS)) for i in range(SLOTS)]
            g_unit = lax.psum(g_unit, "wide", axis_index_groups=same)
        g_unit = lax.all_gather(g_unit, "wide", axis=0, axis_index_groups=slot_groups(wide)).astype(F32)
        g_policy = lax.psum(scatter(g_policy[0]), "wide").astype(F32)
        g_base = lax.psum(scatter(g_base[0]), "wide").astype(F32)
        embed_grad = jnp.sum((pemb[:, :emb] + cemb[:, act : act + emb]).reshape(steps, rows, emb), axis=0)
        table = jnp.einsum("rt,rd->td", onehot[:, :tasks], embed_grad, precision=lax.Precision.HIGHEST)
        slots = jnp.where(jnp.arange(SLOTS)[:, None, None] == slot, unit_vgrad[None], 0.0)
        small = [slots, p_vgrad, c_vgrad, table]
        slots, s_pol, s_chain, grad_table = lax.psum(small, ("wide", "narrow"))
        critics = jnp.stack([g_unit[s] for s in HEAD_SLOT])
        reward = g_unit[REWARD_SLOT]
        c2, c3, c1 = critics[:, :, :feat], critics[:, :, feat : feat + bins], critics[:, :joint, feat + 128 :]
        r2, r3, r1 = reward[:, :feat], reward[:, feat : feat + bins], reward[:joint, feat + 128 :]
        p2, p3, p1 = g_policy[:, :feat], g_policy[:, feat : feat + 2 * act], g_policy[:plain, feat + 128 :]
        d2, e2, d3 = g_base[:, :feat], g_base[:, feat : feat + lat], g_base[:, feat + lat : feat + 2 * lat]
        d1, e1 = g_base[:joint, feat + 2 * lat :], g_base[ublock : ublock + first, feat + 2 * lat :]
        critic_bias_grad = jnp.stack([biases(slots[s]) for s in HEAD_SLOT])
        critic_gain_grad = jnp.stack([gains(slots[s]) for s in HEAD_SLOT])
        reward_rows = slots[REWARD_SLOT]

    return (
        row_loss,
        jnp.swapaxes(z.reshape(steps, rows, lat), 0, 1),
        obs_grad,
        grad_table,
        e1, e2, d1, d2, d3, r1, r2, r3, c1, c2, c3, p1, p2, p3,
        jnp.concatenate([s_chain[0], s_chain[2, :lat]]),
        s_chain[1],
        jnp.concatenate([s_chain[3], s_chain[5], s_chain[7, :lat]]),
        jnp.concatenate([s_chain[4], s_chain[6]]),
        biases(reward_rows),
        gains(reward_rows),
        critic_bias_grad,
        critic_gain_grad,
        jnp.concatenate([s_pol[0], s_pol[2], s_pol[4, : 2 * act]]),
        jnp.concatenate([s_pol[1], s_pol[3]]),
    )


def run_unit(kernel, scalars, units, x, chosen, vec, tile, feat, copies):
    tall, width = x.shape

    def rowed(width):
        return pl.BlockSpec((tile, width), lambda i: (i, 0))

    scratch = pltpu.VMEM((tile, feat), F32)
    early = pl.BlockSpec((tile, width), lambda i: (jnp.minimum(i, 3), 0))
    late = pl.BlockSpec((tile, width), lambda i: (jnp.maximum(i - 4, 0), 0))
    return pl.pallas_call(
        kernel,
        grid=(tall // tile,),
        in_specs=[SMEM] * 3
        + [ANY] * len(units)
        + [rowed(width), rowed(128), pl.BlockSpec(vec.shape, lambda i: (0, 0))],
        out_specs=[early, late, rowed(width)] + [rowed(feat)] * 4 + [rowed(128), pl.BlockSpec((8, feat), lambda i: (0, 0))],
        out_shape=[shape((tall // 2, width), BF16)] * 2
        + [shape((tall, width), BF16)]
        + [shape((tall, feat), BF16)] * 4
        + [shape((tall, 128), BF16), shape((8, feat), F32)],
        scratch_shapes=[
            pltpu.VMEM((width, feat), BF16),
            pltpu.VMEM((feat, feat), BF16),
            pltpu.VMEM((feat, 128), BF16),
        ]
        + [scratch] * 4
        + [pltpu.SemaphoreType.DMA((3 * copies,))],
        compiler_params=pltpu.CompilerParams(vmem_limit_bytes=48 * MIB),
        cost_estimate=pl.CostEstimate(
            flops=8 * tall * feat * feat, bytes_accessed=tall * feat * 12, transcendentals=0
        ),
    )(*scalars, *units, x, chosen, vec)


def solution(mesh):
    both = P(("wide", "narrow"))
    by_row = P("narrow")
    by_head = P(None, "narrow")
    matrices = (by_row,) * 8 + (by_head,) * 3 + (by_row,) * 3
    return jax.shard_map(
        functools.partial(on_device, mesh.shape["wide"], mesh.shape["narrow"]),
        mesh=mesh,
        in_specs=(both,) * 9 + (P(),) + matrices + (P(),) * 10,
        out_specs=(both,) * 3 + (P(),) + matrices + (P(),) * 10,
        check_vma=False,
    )
```

time: 812 us -> 557 us (0.69)
  waiting for transfers between devices: 420 us -> 236 us
  local copies, waits for them, and re-layouts: 130 us -> 64.7 us
  other arithmetic: 70.6 us -> 9.57 us
  Pallas kernels: 90.2 us -> 148 us
  starting transfers between devices: 46.2 us -> 81.4 us
  matrix products: 25.8 us -> 0.14 us
  between operations: 20.7 us -> 6.27 us
    ppermute x16 -> x86, waiting for transfers between devices: 43.6 us -> 192 us  [swap(): return lax.ppermute(array, axis, [(i, i ^ bit) for i in range(size)])]
    unnamed x9 -> x0, waiting for transfers between devices: 137 us -> none
    psum x2 -> x0, waiting for transfers between devices: 102 us -> none  [the longest x1 65.6 us: on_device(): g_base = lax.psum(scatter(g_base), 'wide')]
    all_gather x1 -> x0, waiting for transfers between devices: 74.5 us -> none  [on_device(): lax.all_gather(g_unit, 'wide', axis=0, axis_index_groups=None if wide ==...]
    pallas_call x4 -> x28, Pallas kernels: 90.2 us -> 148 us  [the longest x27 106 us: call(): pl.pallas_call(body, out_shape=list(out_shape), in_specs=[SMEM] * len(sme...]
    ppermute x16 -> x86, starting transfers between devices: 16.1 us -> 63.4 us  [swap(): return lax.ppermute(array, axis, [(i, i ^ bit) for i in range(size)])]
    dot_general x13 -> x1, matrix products: 25.8 us -> 0.14 us  [on_device(): jnp.dot(onehot[:, :tasks], task_table, precision=lax.Precision.HIGHEST)]
    concatenate x18 -> x2, other arithmetic: 21.1 us -> 0.68 us  [the longest x1 0.6 us: on_device(): jnp.concatenate([s_pol[0], s_pol[2], s_pol[4, :2 * act]])]
  transfers between devices with their start and end apart: 34 -> 98, of which waited for: 19 -> 41; matrix products, arithmetic and copies ran while one was open for 16% -> 7% of each run, Pallas kernels for 2% -> 18%
where the time goes in v1:
time: 557 us; the launch traced here: 546 us
  waiting for transfers between devices  236 us (42%)
  Pallas kernels  148 us (27%)
  starting transfers between devices  81.4 us (15%)
  local copies, waits for them, and re-layouts  64.7 us (12%)
  other arithmetic  9.57 us (2%)
  between operations  6.27 us (1%)
    ppermute x86, waiting for transfers between devices, swap(): return lax.ppermute(array, axis, [(i, i ^ bit) for i in range(size)])  192 us
    pallas_call x27, Pallas kernels, call(): pl.pallas_call(body, out_shape=list(out_shape), in_specs=[SMEM] * len(sme...  106 us
    ppermute x86, starting transfers between devices, swap(): return lax.ppermute(array, axis, [(i, i ^ bit) for i in range(size)])  63.4 us
    ppermute x12, waiting for transfers between devices, shift(): lax.ppermute(array, axis, [(i, i + by) for i in range(size) if i // 2 in...  44.1 us
    pallas_call x1, Pallas kernels, run_unit(): pl.pallas_call(kernel, grid=(tall // tile,), in_specs=[SMEM] * 3 + [ANY]...  42.8 us
    unnamed x246, local copies, waits for them, and re-layouts  40.2 us
    ppermute x12, starting transfers between devices, shift(): lax.ppermute(array, axis, [(i, i + by) for i in range(size) if i // 2 in...  18 us
  transfers between devices with their start and end apart: 98, of which 41 were waited for; matrix products, arithmetic and copies ran while one was open for 7% of the time, Pallas kernels for 18%

profile of v1, /device:TPU:0, one launch (start us, length us, event | category | flops | bytes accessed | tf_op | source)
XLA Modules:
  0.0 546.3 jit_solution(3322523092456524897)
XLA Ops:
  26.0 6.3 %collective-permute-done.1.refs_3_ = bf16[128,3584]{1,0:T(8,128)(2,1)S(1)} collective-permute-done((bf16[128,3584]{1,0:T(8,128)(2,1)}, bf16[128,3584]{1,0:T(8,128)(2,1)S(1)}, u32[]{:S(2)}, u32[]{:S(2)}) %collective-permute-start.1) | collective-permute-done | bytes 917536 | tf_op jit(solution)/shard_map/ppermute | solution.py:712
  52.6 9.7 %collective-permute-done.9.refs_3_.refs_8_ = bf16[128,2176]{1,0:T(8,128)(2,1)S(1)} collective-permute-done((bf16[128,2176]{1,0:T(8,128)(2,1)S(1)}, bf16[128,2176]{1,0:T(8,128)(2,1)S(1)}, u32[]{:S(2)}, u32[]{:S(2)}) %collective-permute-start.9) | collective-permute-done | bytes 557088 | tf_op jit(solution)/shard_map/ppermute | solution.py:712
  82.3 18.0 %shard_map.565 = (bf16[288,1024]{1,0:T(8,128)(2,1)S(1)}, bf16[240,896]{1,0:T(8,128)(2,1)}, f32[48,768]{1,0:T(8,128)S(1)}, f32[240,768]{1,0:T(8,128)}, f32[240,1]...) custom-call(s32[9]{0:T(128)S(1)} %stack.244.refs_0_, ...), custom_call_target="tpu_custom_call" | custom-call | flops 1509949440 | bytes 15653888 | tf_op jit(solution)/shard_map/pallas_call | solution.py:37
  128.1 7.2 %shard_map.567 = (bf16[240,1024]{1,0:T(8,128)(2,1)S(1)}, bf16[240,128]{1,0:T(8,128)(2,1)S(1)}, f32[240,1]{1,0:T(8,128)S(1)}, bf16[240,1024]{1,0:T(8,128)(2,1)S(1...) custom-call(s32[9]{0:T(128)S(1)} %stack.244.refs_0_, ...), custom_call_target="tpu_custom_call" | custom-call | flops 1006632960 | bytes 11307840 | tf_op jit(solution)/shard_map/pallas_call | solution.py:37
  154.7 7.8 %collective-permute-done.25 = bf16[240,896]{1,0:T(8,128)(2,1)S(1)} collective-permute-done((bf16[240,896]{1,0:T(8,128)(2,1)S(1)}, bf16[240,896]{1,0:T(8,128)(2,1)S(1)}, u32[]{:S(2)}, u32[]{:S(2)}) %collective-permute-start.25) | collective-permute-done | bytes 430112 | tf_op jit(solution)/shard_map/ppermute | solution.py:712
  167.8 10.1 %collective-permute-done.19.refs_7_ = bf16[128,2176]{1,0:T(8,128)(2,1)S(1)} collective-permute-done((bf16[128,2176]{1,0:T(8,128)(2,1)S(1)}, bf16[128,2176]{1,0:T(8,128)(2,1)S(1)}, u32[]{:S(2)}, u32[]{:S(2)}) %collective-permute-start.19) | collective-permute-done | bytes 557088 | tf_op jit(solution)/shard_map/ppermute | solution.py:712
  178.8 42.8 %shard_map.569 = (bf16[960,896]{1,0:T(8,128)(2,1)}, bf16[960,896]{1,0:T(8,128)(2,1)}, bf16[1920,896]{1,0:T(8,128)(2,1)}, bf16[1920,1024]{1,0:T(8,128)(2,1)}, bf1...) custom-call(f32[3]{0:T(128)S(1)} %pad_maximum_fusion.17.refs_0_, ...), custom_call_target="tpu_custom_call" | custom-call | flops 16106127360 | bytes 23592960 | tf_op jit(solution)/shard_map/pallas_call | solution.py:1147
  221.6 16.2 %shard_map.581 = (bf16[2,128,2176]{2,1,0:T(8,128)(2,1)S(1)}, bf16[2,128,2176]{2,1,0:T(8,128)(2,1)S(1)}, bf16[128,2176]{1,0:T(8,128)(2,1)S(1)}, bf16[128,2176]{1,0:T(8,128)(2,1)S(1)}, bf16[2,128,2176]{2,1,0:T(8,128)(2,1)S(1)}) custom-call(s32[4]{0:T(128)S(1)} %get-tuple-element.311.refs_0_, bf16[1920,896]{1,0:T(8,128)(2,1)} %get-tuple-element.205.refs_1_, ...), custom_call_target="tpu_custom_call" | custom-call | flops 8053063680 | bytes 24150016 | tf_op jit(solution)/shard_map/pallas_call | solution.py:37
  239.5 25.3 %collective-permute-done.53.refs_2_.refs_1_ = bf16[2,128,2176]{2,1,0:T(8,128)(2,1)S(1)} collective-permute-done((bf16[2,128,2176]{2,1,0:T(8,128)(2,1)S(1)}, bf16[2,128,2176]{2,1,0:T(8,128)(2,1)S(1)}, u32[]{:S(2)}, u32[]{:S(2)}) %collective-permute-start.53) | collective-permute-done | bytes 1114144 | tf_op jit(solution)/shard_map/ppermute | solution.py:712
  270.9 10.8 %collective-permute-done.35.refs_1_ = bf16[240,896]{1,0:T(8,128)(2,1)S(1)} collective-permute-done((bf16[240,896]{1,0:T(8,128)(2,1)S(1)}, bf16[240,896]{1,0:T(8,128)(2,1)S(1)}, u32[]{:S(2)}, u32[]{:S(2)}) %collective-permute-start.35) | collective-permute-done | bytes 430112 | tf_op jit(solution)/shard_map/ppermute | solution.py:712
  281.8 6.5 %collective-permute-start.36 = (bf16[240,896]{1,0:T(8,128)(2,1)S(1)}, bf16[240,896]{1,0:T(8,128)(2,1)S(1)}, u32[]{:S(2)}, u32[]{:S(2)}) collective-permute-start(bf16[240,896]{1,0:T(8,128)(2,1)S(1)} %shard_map.571), channel_id=1, source_target_pairs={{0,16},{4,20},{8,24},{12,28},{16,0},{20,4},{24,8},{28,12},{1,17},{... | collective-permute-start | bytes 1290248 | tf_op jit(solution)/shard_map/ppermute | solution.py:712
  295.3 10.8 %collective-permute-done.36.refs_11_ = bf16[240,896]{1,0:T(8,128)(2,1)S(1)} collective-permute-done((bf16[240,896]{1,0:T(8,128)(2,1)S(1)}, bf16[240,896]{1,0:T(8,128)(2,1)S(1)}, u32[]{:S(2)}, u32[]{:S(2)}) %collective-permute-start.36) | collective-permute-done | bytes 430112 | tf_op jit(solution)/shard_map/ppermute | solution.py:712
  307.0 7.8 %shard_map.572 = (f32[240,896]{1,0:T(8,128)}, bf16[240,1024]{1,0:T(8,128)(2,1)S(1)}, bf16[240,1024]{1,0:T(8,128)(2,1)S(1)}, bf16[240,128]{1,0:T(8,128)(2,1)S(1)}...) custom-call(s32[9]{0:T(128)S(1)} %stack.244.refs_0_, bf16[256,2176]{1,0:T(8,128)(2,1)} %copy-done.3, ...), custom_call_target="tpu_custom_call" | custom-call | flops 1006632960 | bytes 12176192 | tf_op jit(solution)/shard_map/pallas_call | solution.py:37
  314.9 19.4 %shard_map.573 = (bf16[288,1024]{1,0:T(8,128)(2,1)S(1)}, bf16[240,1024]{1,0:T(8,128)(2,1)S(1)}, bf16[240,768]{1,0:T(8,128)(2,1)S(1)}, bf16[48,768]{1,0:T(8,128)(...) custom-call(s32[9]{0:T(128)S(1)} %stack.244.refs_0_, bf16[256,3584]{1,0:T(8,128)(2,1)} %copy-done.2, ...), custom_call_target="tpu_custom_call" | custom-call | flops 1509949440 | bytes 16042048 | tf_op jit(solution)/shard_map/pallas_call | solution.py:37
  345.7 13.9 %collective-permute-done.65.refs_11_ = bf16[128,2176]{1,0:T(8,128)(2,1)S(1)} collective-permute-done((bf16[128,2176]{1,0:T(8,128)(2,1)S(1)}, bf16[128,2176]{1,0:T(8,128)(2,1)S(1)}, u32[]{:S(2)}, u32[]{:S(2)}) %collective-permute-start.65) | collective-permute-done | bytes 557088 | tf_op jit(solution)/shard_map/ppermute | solution.py:716
  363.0 12.6 %collective-permute-done.66.refs_12_ = bf16[128,2176]{1,0:T(8,128)(2,1)S(1)} collective-permute-done((bf16[128,2176]{1,0:T(8,128)(2,1)S(1)}, bf16[128,2176]{1,0:T(8,128)(2,1)S(1)}, u32[]{:S(2)}, u32[]{:S(2)}) %collective-permute-start.66) | collective-permute-done | bytes 557088 | tf_op jit(solution)/shard_map/ppermute | solution.py:716
  379.8 10.9 %collective-permute-done.67.refs_13_ = bf16[128,2176]{1,0:T(8,128)(2,1)S(1)} collective-permute-done((bf16[128,2176]{1,0:T(8,128)(2,1)S(1)}, bf16[128,2176]{1,0:T(8,128)(2,1)S(1)}, u32[]{:S(2)}, u32[]{:S(2)}) %collective-permute-start.67) | collective-permute-done | bytes 557088 | tf_op jit(solution)/shard_map/ppermute | solution.py:716
  398.2 6.7 %collective-permute-done.68.refs_14_ = bf16[128,2176]{1,0:T(8,128)(2,1)} collective-permute-done((bf16[128,2176]{1,0:T(8,128)(2,1)S(1)}, bf16[128,2176]{1,0:T(8,128)(2,1)}, u32[]{:S(2)}, u32[]{:S(2)}) %collective-permute-start.68) | collective-permute-done | bytes 557088 | tf_op jit(solution)/shard_map/ppermute | solution.py:716
  418.3 8.2 %shard_map.584 = (f32[5,256,1024]{2,1,0:T(8,128)}, f32[5,256,101]{2,1,0:T(8,128)}, f32[5,218,1024]{2,1,0:T(8,128)}, f32[256,1024]{1,0:T(8,128)}, f32[256,101]{1,...) custom-call(s32[12]{0:T(128)S(1)} %stack.257.refs_0_, bf16[128,2176]{1,0:T(8,128)(2,1)S(1)} %copy-done.20, ...), custom_call_target="tpu_custom_call" | custom-call | bytes 28260352 | tf_op jit(solution)/shard_map/pallas_call | solution.py:37
  437.3 17.4 %collective-permute-done.39.refs_2_ = bf16[2,64,3712]{2,1,0:T(8,128)(2,1)S(1)} collective-permute-done((bf16[2,64,3712]{2,1,0:T(8,128)(2,1)S(1)}, bf16[2,64,3712]{2,1,0:T(8,128)(2,1)S(1)}, u32[]{:S(2)}, u32[]{:S(2)}) %collective-permute-start.39) | collective-permute-done | bytes 950304 | tf_op jit(solution)/shard_map/ppermute | solution.py:712
  459.2 7.4 %collective-permute-done.84.refs_2_ = bf16[2,64,2176]{2,1,0:T(8,128)(2,1)S(1)} collective-permute-done((bf16[2,64,2176]{2,1,0:T(8,128)(2,1)S(1)}, bf16[2,64,2176]{2,1,0:T(8,128)(2,1)S(1)}, u32[]{:S(2)}, u32[]{:S(2)}) %collective-permute-start.84) | collective-permute-done | bytes 557088 | tf_op jit(solution)/shard_map/ppermute | solution.py:712
  470.4 11.5 %collective-permute-done.86.refs_4_ = bf16[64,2176]{1,0:T(8,128)(2,1)S(1)} collective-permute-done((bf16[64,2176]{1,0:T(8,128)(2,1)S(1)}, bf16[64,2176]{1,0:T(8,128)(2,1)S(1)}, u32[]{:S(2)}, u32[]{:S(2)}) %collective-permute-start.86) | collective-permute-done | bytes 278560 | tf_op jit(solution)/shard_map/ppermute | solution.py:712
  498.9 6.6 %collective-permute-done.90.refs_2_ = bf16[32,2176]{1,0:T(8,128)(2,1)S(1)} collective-permute-done((bf16[32,2176]{1,0:T(8,128)(2,1)S(1)}, bf16[32,2176]{1,0:T(8,128)(2,1)S(1)}, u32[]{:S(2)}, u32[]{:S(2)}) %collective-permute-start.90) | collective-permute-done | bytes 139296 | tf_op jit(solution)/shard_map/ppermute | solution.py:712
  509.5 7.5 %collective-permute-done.92.refs_3_ = bf16[32,2176]{1,0:T(8,128)(2,1)S(1)} collective-permute-done((bf16[32,2176]{1,0:T(8,128)(2,1)S(1)}, bf16[32,2176]{1,0:T(8,128)(2,1)S(1)}, u32[]{:S(2)}, u32[]{:S(2)}) %collective-permute-start.92) | collective-permute-done | bytes 139296 | tf_op jit(solution)/shard_map/ppermute | solution.py:712
  (552 shorter events, 238.5 us)
Async XLA Ops:
  51.5 28.9 %collective-permute-start.4 = (bf16[128,3584]{1,0:T(8,128)(2,1)}, bf16[128,3584]{1,0:T(8,128)(2,1)}, u32[]{:S(2)}, u32[]{:S(2)}) collective-permute-start(bf16[128,3584]{1,0:T(8,128)(2,1)} %collective-permute-done.refs_2_), channel_id=1, source_target_pairs={{0,4},{4,0},{8,12},{12,8},{16,20},{20,16},{24,28},{28,24},{1,5},{5... | collective-permute-start | bytes 2752520 | tf_op jit(solution)/shard_map/ppermute | solution.py:712
  69.1 39.3 %collective-permute-start.10 = (bf16[64,2176]{1,0:T(8,128)(2,1)}, bf16[64,2176]{1,0:T(8,128)(2,1)}, u32[]{:S(2)}, u32[]{:S(2)}) collective-permute-start(bf16[64,2176]{1,0:T(8,128)(2,1)} %slice.362), channel_id=1, source_target_pairs={{0,2},{1,3},{2,0},{3,1},{4,6},{5,7},{6,4},{7,5},{8,10},{9,11},{10,... | collective-permute-start | bytes 835592 | tf_op jit(solution)/shard_map/ppermute | solution.py:712
  69.7 57.9 %collective-permute-start.13 = (bf16[128,2176]{1,0:T(8,128)(2,1)S(1)}, bf16[128,2176]{1,0:T(8,128)(2,1)S(1)}, u32[]{:S(2)}, u32[]{:S(2)}) collective-permute-start(bf16[128,2176]{1,0:T(8,128)(2,1)S(1)} %collective-permute-done.9.refs_3_.refs_8_), channel_id=1, source_target_pairs={{0,4},{4,0},{8,12},{12,8},{16,20},{20,16},{24,28},{28,24},{1,5},{5... | collective-permute-start | bytes 1671176 | tf_op jit(solution)/shard_map/ppermute | solution.py:712
  69.8 58.4 %collective-permute-start.12 = (bf16[128,2176]{1,0:T(8,128)(2,1)S(1)}, bf16[128,2176]{1,0:T(8,128)(2,1)}, u32[]{:S(2)}, u32[]{:S(2)}) collective-permute-start(bf16[128,2176]{1,0:T(8,128)(2,1)S(1)} %collective-permute-done.8.refs_2_.refs_7_), channel_id=1, source_target_pairs={{0,4},{4,0},{8,12},{12,8},{16,20},{20,16},{24,28},{28,24},{1,5},{5... | collective-permute-start | bytes 1671176 | tf_op jit(solution)/shard_map/ppermute | solution.py:712
  74.8 42.1 %collective-permute-start.15 = (bf16[64,2176]{1,0:T(8,128)(2,1)}, bf16[64,2176]{1,0:T(8,128)(2,1)}, u32[]{:S(2)}, u32[]{:S(2)}) collective-permute-start(bf16[64,2176]{1,0:T(8,128)(2,1)} %collective-permute-done.11.refs_5_), channel_id=1, source_target_pairs={{0,4},{4,0},{8,12},{12,8},{16,20},{20,16},{24,28},{28,24},{1,5},{5... | collective-permute-start | bytes 835592 | tf_op jit(solution)/shard_map/ppermute | solution.py:712
  108.0 27.9 %collective-permute-start.20 = (bf16[240,896]{1,0:T(8,128)(2,1)}, bf16[240,896]{1,0:T(8,128)(2,1)}, u32[]{:S(2)}, u32[]{:S(2)}) collective-permute-start(bf16[240,896]{1,0:T(8,128)(2,1)} %get-tuple-element.148), channel_id=1, source_target_pairs={{0,4},{4,0},{8,12},{12,8},{16,20},{20,16},{24,28},{28,24},{1,5},{5... | collective-permute-start | bytes 1290248 | tf_op jit(solution)/shard_map/ppermute | solution.py:712
  125.9 27.3 %collective-permute-start.23 = (bf16[240,896]{1,0:T(8,128)(2,1)}, bf16[240,896]{1,0:T(8,128)(2,1)S(1)}, u32[]{:S(2)}, u32[]{:S(2)}) collective-permute-start(bf16[240,896]{1,0:T(8,128)(2,1)} %get-tuple-element.148), channel_id=1, source_target_pairs={{0,8},{4,12},{8,0},{12,4},{16,24},{20,28},{24,16},{28,20},{1,9},{5... | collective-permute-start | bytes 1290248 | tf_op jit(solution)/shard_map/ppermute | solution.py:712
  127.6 35.1 %collective-permute-start.17 = (bf16[256,2176]{1,0:T(8,128)(2,1)S(1)}, bf16[256,2176]{1,0:T(8,128)(2,1)S(1)}, u32[]{:S(2)}, u32[]{:S(2)}) collective-permute-start(bf16[256,2176]{1,0:T(8,128)(2,1)S(1)} %shard_map.568.refs_3_), channel_id=1, source_target_pairs={{0,2},{1,3},{2,0},{3,1},{4,6},{5,7},{6,4},{7,5},{8,10},{9,11},{10,... | collective-permute-start | bytes 3342344 | tf_op jit(solution)/shard_map/ppermute | solution.py:712
  140.0 25.7 %collective-permute-start.16 = (bf16[256,2176]{1,0:T(8,128)(2,1)S(1)}, bf16[256,2176]{1,0:T(8,128)(2,1)S(1)}, u32[]{:S(2)}, u32[]{:S(2)}) collective-permute-start(bf16[256,2176]{1,0:T(8,128)(2,1)S(1)} %shard_map.568.refs_3_), channel_id=1, source_target_pairs={{0,1},{1,0},{2,3},{3,2},{4,5},{5,4},{6,7},{7,6},{8,9},{9,8},{10,11... | collective-permute-start | bytes 3342344 | tf_op jit(solution)/shard_map/ppermute | solution.py:712
  221.5 46.3 %collective-permute-start.34 = (bf16[960,896]{1,0:T(8,128)(2,1)}, bf16[960,896]{1,0:T(8,128)(2,1)S(1)}, u32[]{:S(2)}, u32[]{:S(2)}) collective-permute-start(bf16[960,896]{1,0:T(8,128)(2,1)} %get-tuple-element.151), channel_id=1, source_target_pairs={{0,4},{4,0},{8,12},{12,8},{16,20},{20,16},{24,28},{28,24},{1,5},{5... | collective-permute-start | bytes 5160968 | tf_op jit(solution)/shard_map/ppermute | solution.py:712
  237.8 27.0 %collective-permute-start.53 = (bf16[2,128,2176]{2,1,0:T(8,128)(2,1)S(1)}, bf16[2,128,2176]{2,1,0:T(8,128)(2,1)S(1)}, u32[]{:S(2)}, u32[]{:S(2)}) collective-permute-start(bf16[2,128,2176]{2,1,0:T(8,128)(2,1)S(1)} %get-tuple-element.213), channel_id=1, source_target_pairs={{0,1},{1,0},{2,3},{3,2},{4,5},{5,4},{6,7},{7,6},{8,9},{9,8},{10,11... | collective-permute-start | bytes 3342344 | tf_op jit(solution)/shard_map/ppermute | solution.py:712
  238.8 26.7 %collective-permute-start.54 = (bf16[2,128,2176]{2,1,0:T(8,128)(2,1)S(1)}, bf16[2,128,2176]{2,1,0:T(8,128)(2,1)S(1)}, u32[]{:S(2)}, u32[]{:S(2)}) collective-permute-start(bf16[2,128,2176]{2,1,0:T(8,128)(2,1)S(1)} %get-tuple-element.214), channel_id=1, source_target_pairs={{0,2},{1,3},{2,0},{3,1},{4,6},{5,7},{6,4},{7,5},{8,10},{9,11},{10,... | collective-permute-start | bytes 3342344 | tf_op jit(solution)/shard_map/ppermute | solution.py:712
  269.9 25.3 %collective-permute-start.37 = (bf16[240,896]{1,0:T(8,128)(2,1)}, bf16[240,896]{1,0:T(8,128)(2,1)S(1)}, u32[]{:S(2)}, u32[]{:S(2)}) collective-permute-start(bf16[240,896]{1,0:T(8,128)(2,1)} %get-tuple-element.155), channel_id=1, source_target_pairs={{0,8},{4,12},{8,0},{12,4},{16,24},{20,28},{24,16},{28,20},{1,9},{5... | collective-permute-start | bytes 1290248 | tf_op jit(solution)/shard_map/ppermute | solution.py:712
  288.7 45.6 %collective-permute-start.69 = (bf16[128,2176]{1,0:T(8,128)(2,1)S(1)}, bf16[128,2176]{1,0:T(8,128)(2,1)S(1)}, u32[]{:S(2)}, u32[]{:S(2)}) collective-permute-start(bf16[128,2176]{1,0:T(8,128)(2,1)S(1)} %get-tuple-element.219.refs_1_), channel_id=1, source_target_pairs={{0,4},{4,0},{8,12},{12,8},{16,20},{20,16},{24,28},{28,24},{1,5},{5... | collective-permute-start | bytes 1671176 | tf_op jit(solution)/shard_map/ppermute | solution.py:712
  288.8 47.3 %collective-permute-start.63 = (bf16[128,2176]{1,0:T(8,128)(2,1)S(1)}, bf16[128,2176]{1,0:T(8,128)(2,1)S(1)}, u32[]{:S(2)}, u32[]{:S(2)}) collective-permute-start(bf16[128,2176]{1,0:T(8,128)(2,1)S(1)} %get-tuple-element.219.refs_1_), channel_id=1, source_target_pairs={{16,8},{20,12},{24,16},{28,20},{17,9},{21,13},{25,17},{29,21},{18,... | collective-permute-start | bytes 1671176 | tf_op jit(solution)/shard_map/ppermute | solution.py:716
  289.5 53.0 %collective-permute-start.57 = (bf16[128,2176]{1,0:T(8,128)(2,1)S(1)}, bf16[128,2176]{1,0:T(8,128)(2,1)S(1)}, u32[]{:S(2)}, u32[]{:S(2)}) collective-permute-start(bf16[128,2176]{1,0:T(8,128)(2,1)S(1)} %get-tuple-element.219.refs_1_), channel_id=1, source_target_pairs={{0,8},{4,12},{16,24},{20,28},{1,9},{5,13},{17,25},{21,29},{2,10},{... | collective-permute-start | bytes 1671176 | tf_op jit(solution)/shard_map/ppermute | solution.py:716
  295.2 47.8 %collective-permute-start.70 = (bf16[128,2176]{1,0:T(8,128)(2,1)S(1)}, bf16[128,2176]{1,0:T(8,128)(2,1)S(1)}, u32[]{:S(2)}, u32[]{:S(2)}) collective-permute-start(bf16[128,2176]{1,0:T(8,128)(2,1)S(1)} %get-tuple-element.220.refs_2_), channel_id=1, source_target_pairs={{0,4},{4,0},{8,12},{12,8},{16,20},{20,16},{24,28},{28,24},{1,5},{5... | collective-permute-start | bytes 1671176 | tf_op jit(solution)/shard_map/ppermute | solution.py:712
  306.2 38.2 %collective-permute-start.64 = (bf16[128,2176]{1,0:T(8,128)(2,1)S(1)}, bf16[128,2176]{1,0:T(8,128)(2,1)S(1)}, u32[]{:S(2)}, u32[]{:S(2)}) collective-permute-start(bf16[128,2176]{1,0:T(8,128)(2,1)S(1)} %get-tuple-element.220.refs_2_), channel_id=1, source_target_pairs={{16,8},{20,12},{24,16},{28,20},{17,9},{21,13},{25,17},{29,21},{18,... | collective-permute-start | bytes 1671176 | tf_op jit(solution)/shard_map/ppermute | solution.py:716
  342.5 84.1 %collective-permute-start.38 = (bf16[8,64,3712]{2,1,0:T(8,128)(2,1)}, bf16[8,64,3712]{2,1,0:T(8,128)(2,1)}, u32[]{:S(2)}, u32[]{:S(2)}) collective-permute-start(bf16[8,64,3712]{2,1,0:T(8,128)(2,1)} %get-tuple-element.187), channel_id=1, source_target_pairs={{0,4},{4,0},{8,12},{12,8},{16,20},{20,16},{24,28},{28,24},{1,5},{5... | collective-permute-start | bytes 11403272 | tf_op jit(solution)/shard_map/ppermute | solution.py:712
  404.9 28.5 %collective-permute-start.83 = (bf16[8,64,2176]{2,1,0:T(8,128)(2,1)}, bf16[8,64,2176]{2,1,0:T(8,128)(2,1)}, u32[]{:S(2)}, u32[]{:S(2)}) collective-permute-start(bf16[8,64,2176]{2,1,0:T(8,128)(2,1)} %get-tuple-element.235), channel_id=1, source_target_pairs={{0,4},{4,0},{8,12},{12,8},{16,20},{20,16},{24,28},{28,24},{1,5},{5... | collective-permute-start | bytes 6684680 | tf_op jit(solution)/shard_map/ppermute | solution.py:712
  435.8 30.8 %collective-permute-start.84 = (bf16[2,64,2176]{2,1,0:T(8,128)(2,1)S(1)}, bf16[2,64,2176]{2,1,0:T(8,128)(2,1)S(1)}, u32[]{:S(2)}, u32[]{:S(2)}) collective-permute-start(bf16[2,64,2176]{2,1,0:T(8,128)(2,1)S(1)} %get-tuple-element.237), channel_id=1, source_target_pairs={{0,1},{1,0},{2,3},{3,2},{4,5},{5,4},{6,7},{7,6},{8,9},{9,8},{10,11... | collective-permute-start | bytes 1671176 | tf_op jit(solution)/shard_map/ppermute | solution.py:712
  436.8 30.9 %collective-permute-start.85 = (bf16[2,64,2176]{2,1,0:T(8,128)(2,1)S(1)}, bf16[2,64,2176]{2,1,0:T(8,128)(2,1)S(1)}, u32[]{:S(2)}, u32[]{:S(2)}) collective-permute-start(bf16[2,64,2176]{2,1,0:T(8,128)(2,1)S(1)} %get-tuple-element.238), channel_id=1, source_target_pairs={{0,2},{1,3},{2,0},{3,1},{4,6},{5,7},{6,4},{7,5},{8,10},{9,11},{10,... | collective-permute-start | bytes 1671176 | tf_op jit(solution)/shard_map/ppermute | solution.py:712
  456.0 27.7 %collective-permute-start.41 = (bf16[64,3712]{1,0:T(8,128)(2,1)S(1)}, bf16[64,3712]{1,0:T(8,128)(2,1)S(1)}, u32[]{:S(2)}, u32[]{:S(2)}) collective-permute-start(bf16[64,3712]{1,0:T(8,128)(2,1)S(1)} %get-tuple-element.193), channel_id=1, source_target_pairs={{0,1},{1,0},{2,3},{3,2},{4,5},{5,4},{6,7},{7,6},{8,9},{9,8},{10,11... | collective-permute-start | bytes 1425416 | tf_op jit(solution)/shard_map/ppermute | solution.py:712
  457.0 26.7 %collective-permute-start.42 = (bf16[64,3712]{1,0:T(8,128)(2,1)S(1)}, bf16[64,3712]{1,0:T(8,128)(2,1)S(1)}, u32[]{:S(2)}, u32[]{:S(2)}) collective-permute-start(bf16[64,3712]{1,0:T(8,128)(2,1)S(1)} %get-tuple-element.194), channel_id=1, source_target_pairs={{0,2},{1,3},{2,0},{3,1},{4,6},{5,7},{6,4},{7,5},{8,10},{9,11},{10,... | collective-permute-start | bytes 1425416 | tf_op jit(solution)/shard_map/ppermute | solution.py:712
  (188 other events, 3712.4 us)
